TPU v7x, 128 devices: a whole 4x4x4 slice. The times are simulated.
128 devices in a mesh: gx: 16 (over x, y), gy: 8 (over z, core).
Axes of the slice: x: 4, y: 4, z: 4, core: 2. Of those that a mesh axis runs over, the one named last changes fastest.
Arguments:
- hydro_old: float32 [8, 144, 27, 4096], P('gy', 'gx'), may hold values from -0.8 to 0.8
- phase_old: float32 [8, 144, 15, 4096], P('gy', 'gx'), may hold values from -0.8 to 0.8
- targets: int32 [8, 144], P('gy', 'gx'), may hold values from -1 to 127, as said below
- flags: int32 [8, 144], P('gy', 'gx'), may hold values 0 or 1
- relax_rates: float32 [27], replicated, may hold values from 0.8 to 1.8
Outputs:
- hydro_next: float32 [27, 256, 128, 128], P(None, 'gx', 'gy')
- phase_next: float32 [15, 256, 128, 128], P(None, 'gx', 'gy')
Inputs may be any that keep to these rules, and one draw needn't show every extreme that they name: `targets`: in each row every value 0 to 127 appears exactly once, the rest of the slots are -1 (their populations and flags are unused). No device sends more than 2 blocks to one device of its row, a bound reached in every row; in every row some device holds 9 blocks.
All inputs are finite; a program needn't handle non-finite values. No bound on the sum of `flags` on one device may be relied on, other than what follows from the above.
Results may differ from a plain program's by a relative error of at most 0.0003.
Values sent between devices are 32-bit elements; how exact they have to be, the bound alone decides.
No kernel may reach another device: no remote copies, remote signals or barrier semaphores. Data moves between devices by JAX's collectives and lax.ppermute only.
A program may use at most 192 MiB of HBM per device.

v0:
```python
import jax
import jax.numpy as jnp
import numpy as np
from jax import lax
from jax.sharding import PartitionSpec as P

BS = 16
BZ = 8
STEPS = 1
MOVE_MOST = 2


def with_halo(shard, sides, width):
    for axis, dim in sides:
        size, length = (lax.axis_size(axis), shard.shape[dim])
        up = [(i, (i + 1) % size) for i in range(size)]
        down = [(j, i) for i, j in up]
        last = lax.slice_in_dim(shard, length - width, length, axis=dim)
        leading = lax.slice_in_dim(shard, 0, width, axis=dim)
        before = lax.ppermute(last, axis, up)
        after = lax.ppermute(leading, axis, down)
        shard = jnp.concatenate([before, shard, after], axis=dim)
    return shard


def lattice_tables():
    full_list = [[a, b, c] for a in (-1, 0, 1) for b in (-1, 0, 1) for c in (-1, 0, 1)]
    level = [abs(row[0]) + abs(row[1]) + abs(row[2]) for row in full_list]
    full_table = [8.0 / 27.0, 2.0 / 27.0, 1.0 / 54.0, 1.0 / 216.0]
    small_table = [2.0 / 9.0, 1.0 / 9.0, 0.0, 1.0 / 72.0]
    full = np.array(full_list, dtype=np.float32)
    full_weight = np.array([full_table[v] for v in level], dtype=np.float32)
    small = np.array([row for row, v in zip(full_list, level) if v != 2], dtype=np.float32)
    small_weight = np.array([small_table[v] for v in level if v != 2], dtype=np.float32)
    single = np.array([[1.0, 1.0, 1.0], [-1.0, 0.0, 1.0], [1.0, 0.0, 1.0]], dtype=np.float32)
    single_inverse = np.array(
        [[0.0, -0.5, 0.5], [1.0, 0.0, -1.0], [0.0, 0.5, 0.5]], dtype=np.float32
    )
    moment = np.kron(np.kron(single, single), single)
    inverse = np.kron(np.kron(single_inverse, single_inverse), single_inverse)
    shear_mask = np.zeros(27, dtype=np.float32)
    shear_mask[[4, 10, 12]] = 1.0
    return (full, full_weight, small, small_weight, moment, inverse, shear_mask)


def expand(table, ndim):
    return jnp.asarray(table).reshape((table.shape[0],) + (1,) * (ndim - 1))


def fluid_velocity(hydro):
    full = lattice_tables()[0]
    return jnp.einsum("qc,q...->c...", jnp.asarray(full), hydro, precision=lax.Precision.HIGHEST)


def collide_hydro(hydro, phase, relax_rates):
    full, full_weight, small, small_weight, moment, inverse, shear_mask = lattice_tables()
    ndim = hydro.ndim
    pressure = jnp.sum(hydro, axis=0)
    velocity = fluid_velocity(hydro)
    along = jnp.einsum(
        "qc,c...->q...", jnp.asarray(full), velocity, precision=lax.Precision.HIGHEST
    )
    speed = jnp.sum(velocity * velocity, axis=0)
    equil = expand(full_weight, ndim) * (pressure + 3.0 * along + 4.5 * along * along - 1.5 * speed)
    clipped = jnp.clip(phase, 0.0, 1.0)
    density = 0.001 + 0.999 * clipped
    dynamic = 1e-05 + 0.09999 * clipped
    shear_rate = 1.0 / (0.5 + 3.0 * dynamic / density)
    mask = expand(shear_mask, ndim)
    rates = relax_rates.reshape((27,) + (1,) * (ndim - 1)) * (1.0 - mask) + mask * shear_rate[None]
    spatial = hydro.shape[1:]
    moments = jnp.dot(
        jnp.asarray(moment), (hydro - equil).reshape(27, -1), precision=lax.Precision.HIGHEST
    )
    scaled = rates * moments.reshape((27,) + spatial)
    back = jnp.dot(jnp.asarray(inverse), scaled.reshape(27, -1), precision=lax.Precision.HIGHEST)
    return hydro - back.reshape(hydro.shape)


def collide_phase(phase_pop, phase, grad, velocity, flag_field):
    small, small_weight = lattice_tables()[2:4]
    ndim = phase_pop.ndim
    length = jnp.sqrt(jnp.sum(grad * grad, axis=0) + 0.25)
    normal = grad / length[None]
    along = jnp.einsum(
        "kc,c...->k...", jnp.asarray(small), velocity, precision=lax.Precision.HIGHEST
    )
    facing = jnp.einsum(
        "kc,c...->k...", jnp.asarray(small), normal, precision=lax.Precision.HIGHEST
    )
    weight = expand(small_weight, ndim)
    equil = (
        weight * phase * (1.0 + 3.0 * along)
        + flag_field * weight * 4.0 * phase * (1.0 - phase) * facing
    )
    return phase_pop - (phase_pop - equil) / 0.7


def phase_gradient(fetch):
    full, full_weight = lattice_tables()[:2]
    parts = [None, None, None]
    for index in range(27):
        offset = [int(v) for v in full[index]]
        if offset == [0, 0, 0]:
            continue
        term = float(3.0 * full_weight[index]) * fetch(offset[0], offset[1], offset[2])
        for axis_index in range(3):
            if offset[axis_index] != 0:
                piece = term if offset[axis_index] > 0 else -term
                parts[axis_index] = (
                    piece if parts[axis_index] is None else parts[axis_index] + piece
                )
    return jnp.stack(parts)


def all_offsets():
    full, small = (lattice_tables()[0], lattice_tables()[2])
    return [tuple((int(v) for v in row)) for row in full] + [
        tuple((int(v) for v in row)) for row in small
    ]


def advect_region(widened, start, extent):
    offsets = all_offsets()
    moved = []
    for index in range(42):
        first, second, third = offsets[index]
        slab = widened[
            index, start - first : start - first + extent, start - second : start - second + extent
        ]
        moved.append(jnp.roll(slab, third, axis=-1))
    return jnp.stack(moved)


def plan_sends(target, width, depth, most):
    count = target.shape[0]
    owner = jnp.where(target >= 0, target // depth, -1)
    order = jnp.arange(count, dtype=jnp.int32)
    earlier = (owner[None, :] == owner[:, None]) & (order[None, :] < order[:, None])
    rank = jnp.sum(earlier.astype(jnp.int32), axis=1)
    slots = jnp.arange(width * most, dtype=jnp.int32)
    match = (
        (owner[None, :] == (slots // most)[:, None])
        & (rank[None, :] == (slots % most)[:, None])
        & (target[None, :] >= 0)
    )
    return (jnp.argmax(match, axis=1).astype(jnp.int32), jnp.any(match, axis=1))


def to_field(blocks, comps, edge, depth):
    shaped = blocks.reshape(depth, comps, edge, edge, edge)
    return shaped.transpose(1, 2, 3, 0, 4).reshape(comps, edge, edge, depth * edge)


def on_device(hydro_old, phase_old, targets, flags, relax_rates):
    edge = BS
    depth = BZ
    most = MOVE_MOST
    width = lax.axis_size("gx")
    old_hydro = hydro_old[0]
    old_phase = phase_old[0]
    target = targets[0]
    picked, valid = plan_sends(target, width, depth, most)
    send_hydro = jnp.take(old_hydro, picked, axis=0)
    send_phase = jnp.take(old_phase, picked, axis=0)
    send_tags = jnp.where(valid, target[picked] % depth, -1).astype(jnp.float32)
    send_flags = flags[0][picked].astype(jnp.float32)
    got_hydro, got_phase, got_tags, got_flags = (
        lax.all_to_all(send_hydro, "gx", split_axis=0, concat_axis=0, tiled=True),
        lax.all_to_all(send_phase, "gx", split_axis=0, concat_axis=0, tiled=True),
        lax.all_to_all(send_tags, "gx", split_axis=0, concat_axis=0, tiled=True),
        lax.all_to_all(send_flags, "gx", split_axis=0, concat_axis=0, tiled=True),
    )
    levels = jnp.arange(depth, dtype=jnp.float32)
    where_from = jnp.argmax(got_tags[None, :] == levels[:, None], axis=1).astype(jnp.int32)
    hydro = to_field(jnp.take(got_hydro, where_from, axis=0), 27, edge, depth)
    phase_pop = to_field(jnp.take(got_phase, where_from, axis=0), 15, edge, depth)
    flag_line = jnp.repeat(jnp.take(got_flags, where_from, axis=0), edge)
    flag_field = jnp.broadcast_to(flag_line, (edge, edge, depth * edge))
    for turn_index in range(STEPS):
        phase = jnp.sum(phase_pop, axis=0)
        padded = with_halo(phase, (("gx", 0), ("gy", 1)), 1)
        grad = phase_gradient(
            lambda a, b, c: jnp.roll(
                padded[1 + a : 1 + a + edge, 1 + b : 1 + b + edge], -c, axis=-1
            )
        )
        velocity = fluid_velocity(hydro)
        hydro_post = collide_hydro(hydro, phase, relax_rates)
        phase_post = collide_phase(phase_pop, phase, grad, velocity, flag_field)
        stacked = jnp.concatenate([hydro_post, phase_post], axis=0)
        widened = with_halo(stacked, (("gx", 1), ("gy", 2)), 1)
        region = advect_region(widened, 1, edge)
        hydro = region[:27]
        phase_pop = region[27:]
    return (hydro, phase_pop)


def solution(mesh):
    in_specs = (
        P("gy", "gx", None, None),
        P("gy", "gx", None, None),
        P("gy", "gx"),
        P("gy", "gx"),
        P(),
    )
    out_specs = (P(None, "gx", "gy", None), P(None, "gx", "gy", None))
    return jax.shard_map(
        on_device, mesh=mesh, in_specs=in_specs, out_specs=out_specs, check_vma=False
    )
```

profile of v0, /device:TPU:29, one launch (start us, length us, event | category | flops | bytes accessed | tf_op | source)
XLA Modules:
  0.0 611.5 jit_solution(15806562550201559405)
XLA Ops:
  6.0 6.6 %all-to-all-start = ((f32[16,2,1]{1,2,0:T(1,128)}), f32[16,2,1]{1,2,0:T(1,128)S(1)}, u32[]{:S(2)}, u32[]{:S(2)}) async-start(f32[16,2,1]{1,2,0:T(1,128)} %copy.370), calls=%async_computation | async-start | bytes 16384 | tf_op jit(solution)/shard_map/all_to_all | solution.py:171
  14.0 3.4 copy.426
  17.4 4.3 gather_fusion.3
  21.7 6.7 %all-to-all-start.3 = ((f32[16,2,1]{1,2,0:T(1,128)}), f32[16,2,1]{1,2,0:T(1,128)S(1)}, u32[]{:S(2)}, u32[]{:S(2)}) async-start(f32[16,2,1]{1,2,0:T(1,128)} %bitcast.12), calls=%async_computation.3 | async-start | bytes 16384 | tf_op jit(solution)/shard_map/all_to_all | solution.py:172
  28.4 8.2 %broadcast_select_fusion.1 = f32[32,15,4096]{2,1,0:T(8,128)} fusion(f32[32,15,4096]{2,1,0:T(8,128)} %gather_fusion.3, pred[32]{0:T(512)(128)(4,1)S(1)} %compare_and_fusion), kind=kLoop, calls=%fused_computation.19 | loop fusion | flops 1966080 | bytes 15728672 | tf_op jit(solution)/shard_map/jit(_take)/select_n | solution.py:165
  36.6 6.7 %all-to-all-start.2 = ((f32[32,15,4096]{2,1,0:T(8,128)}), f32[32,15,4096]{2,1,0:T(8,128)}, u32[]{:S(2)}, u32[]{:S(2)}) async-start(f32[32,15,4096]{2,1,0:T(8,128)} %broadcast_select_fusion.1), calls=%async_computation.2 | async-start | bytes 16777216 | tf_op jit(solution)/shard_map/all_to_all | solution.py:170
  43.2 8.0 %copy.425 = f32[1,9,27,4096]{3,2,0,1:T(8,128)} copy(f32[1,9,27,4096]{3,0,2,1:T(1,128)} %param.14) | data formatting | bytes 7962624
  51.2 10.3 %gather_fusion.1 = f32[32,27,4096]{2,1,0:T(8,128)} fusion(f32[9,27,4096]{2,1,0:T(8,128)} %bitcast.325, s32[1024]{0:T(1024)S(1)} %pad_clamp_fusion.1), kind=kCustom, calls=%fused_computation.1 | custom fusion | bytes 28311680 | tf_op jit(solution)/shard_map/jit(_take)/gather | solution.py:164
  61.6 11.9 %broadcast_select_fusion = f32[32,27,4096]{2,1,0:T(8,128)} fusion(f32[32,27,4096]{2,1,0:T(8,128)} %gather_fusion.1, pred[32]{0:T(512)(128)(4,1)S(1)} %compare_and_fusion), kind=kLoop, calls=%fused_computation.10 | loop fusion | flops 3538944 | bytes 28311584 | tf_op jit(solution)/shard_map/jit(_take)/select_n | solution.py:164
  73.5 103.2 %all-to-all-done.2 = f32[32,15,4096]{2,1,0:T(8,128)} async-done(((f32[32,15,4096]{2,1,0:T(8,128)}), f32[32,15,4096]{2,1,0:T(8,128)}, u32[]{:S(2)}, u32[]{:S(2)}) %all-to-all-start.2) | async-done | bytes 7864352 | tf_op jit(solution)/shard_map/all_to_all | solution.py:170
  176.6 7.0 %all-to-all-start.1 = ((f32[32,27,4096]{2,1,0:T(8,128)}), f32[32,27,4096]{2,1,0:T(8,128)}, u32[]{:S(2)}, u32[]{:S(2)}) async-start(f32[32,27,4096]{2,1,0:T(8,128)} %broadcast_select_fusion), calls=%async_computation.1 | async-start | bytes 33554432 | tf_op jit(solution)/shard_map/all_to_all | solution.py:169
  187.2 4.1 gather_fusion.4
  193.7 9.7 %gather.39 = f32[8,15,16,16,16]{4,3,2,0,1:T(8,128)} reshape(f32[8,15,4096]{2,0,1:T(8,128)} %copy.373) | data formatting | bytes 3932160 | tf_op jit(solution)/shard_map/jit(_take)/gather | solution.py:177
  203.4 11.8 %fusion.151 = (f32[16,16,8,16]{3,1,0,2:T(8,128)S(1)}, f32[15,16,16,8,16]{4,2,1,3,0:T(8,128)}) fusion(f32[8,15,16,16,16]{4,3,2,0,1:T(8,128)} %gather.39, pred[8]{0:T(512)(128)(4,1)S(1)} %get-tuple-element.11), kind=kLoop, calls=%fused_computation.403 | loop fusion | flops 950272 | bytes 4063240 | tf_op jit(solution)/shard_map/reduce_sum | solution.py:181
  220.3 20.0 %copy.410 = f32[15,16,16,8,16]{4,3,0,2,1:T(8,128)} copy(f32[15,16,16,8,16]{4,2,1,3,0:T(8,128)} %get-tuple-element.13) | data formatting | bytes 3932160 | tf_op jit(solution)/shard_map/reshape | solution.py:152
  240.3 11.2 %reshape.908 = f32[15,16,16,128]{3,0,2,1:T(8,128)} reshape(f32[15,16,16,8,16]{4,3,0,2,1:T(8,128)} %copy.410) | data formatting | bytes 3932160 | tf_op jit(solution)/shard_map/reshape | solution.py:152
  251.5 125.3 %collective-permute-done = f32[1,16,128]{2,1,0:T(8,128)S(1)} collective-permute-done((f32[1,16,128]{2,1,0:T(8,128)S(1)}, f32[1,16,128]{2,1,0:T(8,128)S(1)}, u32[]{:S(2)}, u32[]{:S(2)}) %collective-permute-start) | collective-permute-done | bytes 8224 | tf_op jit(solution)/shard_map/ppermute | solution.py:20
  377.6 67.8 %collective-permute-done.1 = f32[1,16,128]{2,1,0:T(8,128)S(1)} collective-permute-done((f32[1,16,128]{2,1,0:T(8,128)S(1)}, f32[1,16,128]{2,1,0:T(8,128)S(1)}, u32[]{:S(2)}, u32[]{:S(2)}) %collective-permute-start.1) | collective-permute-done | bytes 8224 | tf_op jit(solution)/shard_map/ppermute | solution.py:21
  445.3 13.3 %collective-permute-start.3 = (f32[18,1,128]{2,1,0:T(1,128)S(1)}, f32[18,1,128]{2,1,0:T(1,128)S(1)}, u32[]{:S(2)}, u32[]{:S(2)}) collective-permute-start(f32[18,1,128]{2,1,0:T(1,128)S(1)} %get-tuple-element.81), channel_id=1, source_target_pairs={{1,0},{2,1},{3,2},{4,3},{5,4},{6,5},{7,6},{0,7},{9,8},{10,9},{11,1... | collective-permute-start | bytes 27656 | tf_op jit(solution)/shard_map/ppermute | solution.py:21
  464.9 8.5 %gather_fusion.2 = f32[8,27,4096]{2,1,0:T(8,128)} fusion(f32[32,27,4096]{2,1,0:T(8,128)} %all-to-all-done.1, s32[1024]{0:T(1024)S(1)} %pad_clamp_fusion), kind=kCustom, calls=%fused_computation.2 | custom fusion | bytes 7077920 | tf_op jit(solution)/shard_map/jit(_take)/gather | solution.py:176
  473.4 4.2 copy.371
  477.7 13.8 %gather.36 = f32[8,27,16,16,16]{4,3,2,0,1:T(8,128)} reshape(f32[8,27,4096]{2,0,1:T(8,128)S(1)} %copy.371) | data formatting | bytes 7077888 | tf_op jit(solution)/shard_map/jit(_take)/gather | solution.py:176
  491.4 13.5 %fusion.149 = (f32[16,16,8,16]{3,1,0,2:T(8,128)}, f32[27,16,16,8,16]{4,2,1,3,0:T(8,128)S(1)}) fusion(f32[8,27,16,16,16]{4,3,2,0,1:T(8,128)} %gather.36, pred[8]{0:T(512)(128)(4,1)S(1)} %get-tuple-element.11), kind=kLoop, calls=%fused_computation.402 | loop fusion | flops 1736704 | bytes 7208968 | tf_op jit(solution)/shard_map/reduce_sum | solution.py:58
  505.0 18.9 %copy.372 = f32[27,16,16,8,16]{4,3,2,1,0:T(8,128)} copy(f32[27,16,16,8,16]{4,2,1,3,0:T(8,128)S(1)} %get-tuple-element.7) | data formatting | bytes 7077888 | tf_op jit(solution)/shard_map/transpose | solution.py:152
  523.8 17.3 %reshape.833 = f32[27,16,16,128]{3,2,1,0:T(8,128)S(1)} reshape(f32[27,16,16,8,16]{4,3,2,1,0:T(8,128)} %copy.372) | data formatting | bytes 7077888 | tf_op jit(solution)/shard_map/reshape | solution.py:152
  541.2 4.9 multiply_reduce_fusion
  550.5 8.2 %copy_subtract_fusion = f32[27,16,16,128]{3,0,2,1:T(8,128)S(1)} fusion(f32[27,16,16,128]{3,2,1,0:T(8,128)S(1)} %reshape.833, f32[27,3,1,1]{0,1,3,2:T(4,128)S(1)} %copy-done.14, f32[3,16,16,128]{3,0,2,1:T(4,128)} %get-tuple-element.113, f32[16,16,128]{2,1,0:T(8,128)} %broadcast_multiply_fusion.1, f32[16,16,128]{2,1,0:T(8,128)} %add.411, f32[27]{0:T(128)S(1)} %copy-done.18), kind=kOutput, calls=%fused_computation.15 | convolution fusion | flops 38928384 | bytes 7733680 | tf_op jit(solution)/shard_map/qc,c...->q.../dot_general | solution.py:60
  563.7 4.2 convolution_multiply_fusion
  568.0 4.2 fusion.158
  581.4 5.5 collective-permute-done.4
  590.7 3.5 collective-permute-start.6
  596.3 5.5 collective-permute-done.6
  (206 shorter events, 57.9 us)
Async XLA Ops:
  0.6 11.9 %copy-start = (s32[1,9]{1,0:T(1,128)S(1)}, s32[1,9]{1,0:T(1,128)}, u32[]{:S(2)}) copy-start(s32[1,9]{1,0:T(1,128)} %param.17) | copy-start | bytes 112
  6.0 15.7 %all-to-all-start = ((f32[16,2,1]{1,2,0:T(1,128)}), f32[16,2,1]{1,2,0:T(1,128)S(1)}, u32[]{:S(2)}, u32[]{:S(2)}) async-start(f32[16,2,1]{1,2,0:T(1,128)} %copy.370), calls=%async_computation | async-start | bytes 16384 | tf_op jit(solution)/shard_map/all_to_all | solution.py:171
  21.7 14.8 %all-to-all-start.3 = ((f32[16,2,1]{1,2,0:T(1,128)}), f32[16,2,1]{1,2,0:T(1,128)S(1)}, u32[]{:S(2)}, u32[]{:S(2)}) async-start(f32[16,2,1]{1,2,0:T(1,128)} %bitcast.12), calls=%async_computation.3 | async-start | bytes 16384 | tf_op jit(solution)/shard_map/all_to_all | solution.py:172
  36.6 140.1 %all-to-all-start.2 = ((f32[32,15,4096]{2,1,0:T(8,128)}), f32[32,15,4096]{2,1,0:T(8,128)}, u32[]{:S(2)}, u32[]{:S(2)}) async-start(f32[32,15,4096]{2,1,0:T(8,128)} %broadcast_select_fusion.1), calls=%async_computation.2 | async-start | bytes 16777216 | tf_op jit(solution)/shard_map/all_to_all | solution.py:170
  73.5 110.2 %copy-start.19 = (f32[27]{0:T(128)S(1)}, f32[27]{0:T(128)}, u32[]{:S(2)}) copy-start(f32[27]{0:T(128)} %param.18) | copy-start | bytes 328
  73.5 110.2 %copy-start.20 = (f32[27]{0:T(128)S(1)}, f32[27]{0:T(128)}, u32[]{:S(2)}) copy-start(f32[27]{0:T(128)} %constant.195) | copy-start | bytes 328
  176.6 288.3 %all-to-all-start.1 = ((f32[32,27,4096]{2,1,0:T(8,128)}), f32[32,27,4096]{2,1,0:T(8,128)}, u32[]{:S(2)}, u32[]{:S(2)}) async-start(f32[32,27,4096]{2,1,0:T(8,128)} %broadcast_select_fusion), calls=%async_computation.1 | async-start | bytes 33554432 | tf_op jit(solution)/shard_map/all_to_all | solution.py:169
  216.2 160.6 %copy-start.2 = (f32[16,16,128]{2,1,0:T(8,128)}, f32[16,16,128]{2,1,0:T(8,128)S(1)}, u32[]{:S(2)}) copy-start(f32[16,16,128]{2,1,0:T(8,128)S(1)} %mul.411) | copy-start | bytes 393220
  216.3 160.5 %collective-permute-start = (f32[1,16,128]{2,1,0:T(8,128)S(1)}, f32[1,16,128]{2,1,0:T(8,128)S(1)}, u32[]{:S(2)}, u32[]{:S(2)}) collective-permute-start(f32[1,16,128]{2,1,0:T(8,128)S(1)} %slice.557), channel_id=1, source_target_pairs={{0,8},{8,16},{16,24},{24,32},{32,40},{40,48},{48,56},{56,64},{64,7... | collective-permute-start | bytes 24584 | tf_op jit(solution)/shard_map/ppermute | solution.py:20
  219.5 225.8 %collective-permute-start.1 = (f32[1,16,128]{2,1,0:T(8,128)S(1)}, f32[1,16,128]{2,1,0:T(8,128)S(1)}, u32[]{:S(2)}, u32[]{:S(2)}) collective-permute-start(f32[1,16,128]{2,1,0:T(8,128)S(1)} %slice.559), channel_id=1, source_target_pairs={{8,0},{16,8},{24,16},{32,24},{40,32},{48,40},{56,48},{64,56},{72,6... | collective-permute-start | bytes 24584 | tf_op jit(solution)/shard_map/ppermute | solution.py:21
  445.3 16.1 %collective-permute-start.3 = (f32[18,1,128]{2,1,0:T(1,128)S(1)}, f32[18,1,128]{2,1,0:T(1,128)S(1)}, u32[]{:S(2)}, u32[]{:S(2)}) collective-permute-start(f32[18,1,128]{2,1,0:T(1,128)S(1)} %get-tuple-element.81), channel_id=1, source_target_pairs={{1,0},{2,1},{3,2},{4,3},{5,4},{6,5},{7,6},{0,7},{9,8},{10,9},{11,1... | collective-permute-start | bytes 27656 | tf_op jit(solution)/shard_map/ppermute | solution.py:21
  459.0 2.9 collective-permute-start.2
  523.8 17.3 %copy-start.14 = (f32[27,3,1,1]{0,1,3,2:T(4,128)S(1)}, f32[27,3,1,1]{0,1,3,2:T(4,128)}, u32[]{:S(2)}) copy-start(f32[27,3,1,1]{0,1,3,2:T(4,128)} %constant.196) | copy-start | bytes 976
  541.1 5.6 copy-start.5
  541.1 9.3 %copy-start.18 = (f32[27]{0:T(128)S(1)}, f32[27]{0:T(128)}, u32[]{:S(2)}) copy-start(f32[27]{0:T(128)} %constant.184.clone) | copy-start | bytes 328
  561.2 2.5 copy-start.7
  561.2 2.5 copy-start.12
  561.2 2.5 copy-start.17
  563.7 4.3 copy-start.11
  573.3 2.9 copy-start.3
  573.3 2.9 copy-start.6
  573.3 2.9 copy-start.8
  573.3 2.9 copy-start.9
  573.3 2.9 copy-start.10
  573.3 2.9 copy-start.21
  579.9 7.0 %collective-permute-start.4 = (f32[42,1,16,128]{3,2,1,0:T(8,128)S(1)}, f32[42,1,16,128]{3,2,1,0:T(8,128)S(1)}, u32[]{:S(2)}, u32[]{:S(2)}) collective-permute-start(f32[42,1,16,128]{3,2,1,0:T(8,128)S(1)} %get-tuple-element.49), channel_id=1, source_target_pairs={{0,8},{8,16},{16,24},{24,32},{32,40},{40,48},{48,56},{56,64},{64,7... | collective-permute-start | bytes 1032200 | tf_op jit(solution)/shard_map/ppermute | solution.py:20
  580.0 9.1 %collective-permute-start.5 = (f32[42,1,16,128]{3,2,1,0:T(8,128)S(1)}, f32[42,1,16,128]{3,2,1,0:T(8,128)S(1)}, u32[]{:S(2)}, u32[]{:S(2)}) collective-permute-start(f32[42,1,16,128]{3,2,1,0:T(8,128)S(1)} %get-tuple-element.50), channel_id=1, source_target_pairs={{8,0},{16,8},{24,16},{32,24},{40,32},{48,40},{56,48},{64,56},{72,6... | collective-permute-start | bytes 1032200 | tf_op jit(solution)/shard_map/ppermute | solution.py:21
  590.7 11.0 %collective-permute-start.6 = (f32[42,18,1,128]{3,2,1,0:T(1,128)S(1)}, f32[42,18,1,128]{3,2,1,0:T(1,128)S(1)}, u32[]{:S(2)}, u32[]{:S(2)}) collective-permute-start(f32[42,18,1,128]{3,2,1,0:T(1,128)S(1)} %get-tuple-element.41), channel_id=1, source_target_pairs={{1,0},{2,1},{3,2},{4,3},{5,4},{6,5},{7,6},{0,7},{9,8},{10,9},{11,1... | collective-permute-start | bytes 1161224 | tf_op jit(solution)/shard_map/ppermute | solution.py:21
  594.4 7.8 %collective-permute-start.7 = (f32[42,18,1,128]{3,2,1,0:T(1,128)S(1)}, f32[42,18,1,128]{3,2,1,0:T(1,128)S(1)}, u32[]{:S(2)}, u32[]{:S(2)}) collective-permute-start(f32[42,18,1,128]{3,2,1,0:T(1,128)S(1)} %get-tuple-element.40), channel_id=1, source_target_pairs={{0,1},{1,2},{2,3},{3,4},{4,5},{5,6},{6,7},{7,0},{8,9},{9,10},{10,1... | collective-permute-start | bytes 1161224 | tf_op jit(solution)/shard_map/ppermute | solution.py:20
  607.8 3.4 copy-start.1
  608.2 1.3 copy-start.13
  609.5 1.8 copy-start.15
  (2 other events, 2.1 us)
where the time goes:
time: 620 us; the launch traced here: 612 us
  waiting for transfers between devices  310 us (50%)
  local copies, waits for them, and re-layouts  161 us (26%)
  other arithmetic  61.3 us (10%)
  starting transfers between devices  50.4 us (8%)
  matrix products  26.3 us (4%)
    ppermute x4, waiting for transfers between devices, with_halo(): before = lax.ppermute(last, axis, up)  131 us
    all_to_all x1, waiting for transfers between devices, on_device(): lax.all_to_all(send_phase, 'gx', split_axis=0, concat_axis=0, tiled=True)  103 us
    ppermute x4, waiting for transfers between devices, with_halo(): after = lax.ppermute(leading, axis, down)  76.3 us
    reshape x3, local copies, waits for them, and re-layouts, to_field(): shaped.transpose(1, 2, 3, 0, 4).reshape(comps, edge, edge, depth * edge)  48.5 us
    gather x3, local copies, waits for them, and re-layouts, on_device(): hydro = to_field(jnp.take(got_hydro, where_from, axis=0), 27, edge, depth)  26.5 us
    ppermute x4, starting transfers between devices, with_halo(): after = lax.ppermute(leading, axis, down)  19 us
    transpose x1, local copies, waits for them, and re-layouts, to_field(): shaped.transpose(1, 2, 3, 0, 4).reshape(comps, edge, edge, depth * edge)  18.9 us
    unnamed x52, local copies, waits for them, and re-layouts  18.8 us
  transfers between devices with their start and end apart: 12, of which 7 were waited for; matrix products, arithmetic and copies ran while one was open for 19% of the time, Pallas kernels for 0%

commit v1 on v0

v1 whole, which is shorter than its diff:
```python
import functools

import jax
import jax.numpy as jnp
import numpy as np
from jax import lax
from jax.experimental import pallas as pl
from jax.experimental.pallas import tpu as pltpu
from jax.sharding import PartitionSpec as P

BS = 16
BZ = 8
SLOT_ROWS = 88
LANES = 128
VMEM_LIMIT = 56 * 1024 * 1024

FULL = [(a, b, c) for a in (-1, 0, 1) for b in (-1, 0, 1) for c in (-1, 0, 1)]
SMALL = [v for v in FULL if sum(map(abs, v)) != 2]
ORDER = sorted(
    [("h", q, v) for q, v in enumerate(FULL)] + [("p", k, v) for k, v in enumerate(SMALL)],
    key=lambda t: (t[2][0], t[2][1], t[0], t[1]),
)
PLACE = {(kind, index): n for n, (kind, index, _) in enumerate(ORDER)}
UP_FACE = [n for n, t in enumerate(ORDER) if t[2][1] == 1]
DOWN_FACE = [n for n, t in enumerate(ORDER) if t[2][1] == -1]


def runs(places):
    out = []
    for n in places:
        if out and out[-1][1] == n:
            out[-1][1] = n + 1
        else:
            out.append([n, n + 1])
    return out


def pack_kernel(place_ref, h_ref, p_ref, target_ref, flag_ref, out_ref, here_ref):
    step = pl.program_id(0)
    slots = target_ref.shape[1]

    here_ref[0] = place_ref[0]

    @pl.when(step < slots)
    def _():
        for part in range(4):
            rows = pl.ds(part * 8, 8)
            groups = [[h_ref[0, 4 * n + m, rows, :] for m in range(4)] for n in range(6)]
            groups += [[p_ref[0, 4 * n + m, rows, :] for m in range(4)] for n in range(3)]
            last_h = [h_ref[0, 24 + m, rows, :] for m in range(3)]
            last_p = [p_ref[0, 12 + m, rows, :] for m in range(3)]
            groups += [last_p + [beside(p_ref, part, -1)], last_h + [beside(p_ref, part, 1)]]
            for n, group in enumerate(groups):
                for m, value in enumerate(swap_bits(group, 0, 2)):
                    out_ref[part * 4 + m, pl.ds(n * 8, 8), :] = value

    @pl.when(step == slots)
    def _():
        for i in range(BS):
            out_ref[i, 0:1, 0:slots] = target_ref[...].astype(jnp.float32)
            out_ref[i, 1:2, 0:slots] = flag_ref[...].astype(jnp.float32)


def beside(p_ref, part, side):
    near = sum(p_ref[0, k, pl.ds(part * 8, 8), :] for k in range(15))
    other = (part + side) % 4
    far = sum(p_ref[0, k, pl.ds(other * 8, 8), :] for k in range(15))
    row = lax.broadcasted_iota(jnp.int32, (8, LANES), 0)
    if side < 0:
        return jnp.where(row < 2, pltpu.roll(far, 2, 0), pltpu.roll(near, 2, 0))
    return jnp.where(row >= 6, pltpu.roll(far, 6, 0), pltpu.roll(near, 6, 0))


def pack(place, hydro, phase, targets, flags):
    slots = hydro.shape[0]
    whole = pl.BlockSpec(memory_space=pltpu.VMEM)
    return pl.pallas_call(
        pack_kernel,
        grid=(slots + 1,),
        in_specs=[
            pl.BlockSpec(memory_space=pltpu.SMEM),
            pl.BlockSpec((1, 27, 32, LANES), lambda s: (jnp.minimum(s, slots - 1), 0, 0, 0)),
            pl.BlockSpec((1, 15, 32, LANES), lambda s: (jnp.minimum(s, slots - 1), 0, 0, 0)),
            whole,
            whole,
        ],
        out_specs=[
            pl.BlockSpec((BS, SLOT_ROWS, LANES), lambda s: (0, s, 0)),
            pl.BlockSpec(memory_space=pltpu.SMEM),
        ],
        out_shape=[
            jax.ShapeDtypeStruct((BS, slots * SLOT_ROWS + 8, LANES), jnp.float32),
            jax.ShapeDtypeStruct((1,), jnp.int32),
        ],
        compiler_params=pltpu.CompilerParams(vmem_limit_bytes=VMEM_LIMIT),
    )(place, hydro.reshape(slots, 27, 32, LANES), phase.reshape(slots, 15, 32, LANES), targets, flags)


def swap_bits(values, axis, unit):
    count = len(values)
    size = count * unit
    position = lax.broadcasted_iota(jnp.int32, (8, LANES), axis) // unit
    step = 1
    while step < count:
        high = (position & step) != 0
        fresh = list(values)
        for n in range(count):
            if n & step:
                continue
            a, b = values[n], values[n + step]
            fresh[n] = jnp.where(high, pltpu.roll(b, step * unit, axis), a)
            fresh[n + step] = jnp.where(high, b, pltpu.roll(a, size - step * unit, axis))
        values = fresh
        step *= 2
    return values


GROUPS = [[4 * n + m for m in range(4)] for n in range(6)]
GROUPS += [[27 + 4 * n + m for m in range(4)] for n in range(3)]
GROUPS += [[39, 40, 41, 42], [24, 25, 26, 43]]


def spread_kernel(where_ref, *refs):
    blocks, out_ref = refs[:8], refs[8]
    for group in range(SLOT_ROWS // 8):
        values = [blocks[level][0, pl.ds(group * 8, 8), :] for level in range(8)]
        values = swap_bits(values, 1, 16)
        values = swap_bits(values, 0, 1)
        for n in range(8):
            out_ref[0, GROUPS[group][n // 2], pl.ds((n % 2) * 8, 8), :] = values[n]
    total = out_ref[0, 27]
    for k in range(1, 15):
        total = total + out_ref[0, 27 + k]
    out_ref[0, 44] = total


def spread(where, got):
    def block(level):
        return pl.BlockSpec(
            (1, SLOT_ROWS, LANES), lambda d, w: (w[0, d * 8 + level], w[1, d * 8 + level], 0)
        )

    return pl.pallas_call(
        spread_kernel,
        grid_spec=pltpu.PrefetchScalarGridSpec(
            num_scalar_prefetch=1,
            grid=(16,),
            in_specs=[block(level) for level in range(8)],
            out_specs=pl.BlockSpec((1, 45, BS, LANES), lambda d, w: (d, 0, 0, 0)),
        ),
        out_shape=jax.ShapeDtypeStruct((16, 45, BS, LANES), jnp.float32),
        compiler_params=pltpu.CompilerParams(vmem_limit_bytes=VMEM_LIMIT),
    )(where, *([got] * 8))


def to_moments(f):
    f = list(f)
    for stride in (1, 3, 9):
        for n in range(27):
            if (n // stride) % 3 == 0:
                low, mid, high = f[n], f[n + stride], f[n + 2 * stride]
                both = low + high
                f[n], f[n + stride], f[n + 2 * stride] = both + mid, high - low, both
    return f


def from_moments(m):
    m = list(m)
    for stride in (1, 3, 9):
        for n in range(27):
            if (n // stride) % 3 == 0:
                zero, one, two = m[n], m[n + stride], m[n + 2 * stride]
                low, high = two - one, two + one
                m[n], m[n + stride], m[n + 2 * stride] = low, zero - (low + high), high
    return m


def equil_moments(pressure, velocity):
    x, y, z = velocity
    squares = (x * x, y * y, z * z)
    cross = {(1, 1, 0): x * y, (1, 0, 1): x * z, (0, 1, 1): y * z}
    third = pressure * (1.0 / 3.0)
    total = squares[0] + squares[1] + squares[2]
    out = [None] * 27
    for q in range(27):
        powers = (q // 9, q // 3 % 3, q % 3)
        ones = tuple(int(n == 1) for n in powers)
        scale = (1.0 / 3.0) ** sum(n == 2 for n in powers)
        if sum(ones) == 0:
            two = [squares[n] for n in range(3) if powers[n] == 2]
            value = pressure if not two else pressure + 3.0 * sum(two[1:], two[0])
            out[q] = value if scale == 1.0 else scale * value
        elif sum(ones) == 1:
            value = velocity[ones.index(1)]
            out[q] = value if scale == 1.0 else scale * value
        elif sum(ones) == 2:
            out[q] = cross[ones] if scale == 1.0 else scale * cross[ones]
        else:
            out[q] = 0.0
    return out


def weighted(v, table):
    return table[sum(map(abs, v))]


FULL_WEIGHT = [8.0 / 27.0, 2.0 / 27.0, 1.0 / 54.0, 1.0 / 216.0]
SMALL_WEIGHT = [2.0 / 9.0, 1.0 / 9.0, 0.0, 1.0 / 72.0]


def dot(v, parts):
    total = None
    for c, part in zip(v, parts):
        if c != 0:
            if total is None:
                total = part if c > 0 else -part
            else:
                total = total + part if c > 0 else total - part
    return total


def collide_kernel(place_ref, rate_ref, n_ref, before_ref, after_ref, low_ref, high_ref, flag_ref, out_ref):
    d = pl.program_id(0)
    place = place_ref[0]
    left = jnp.where(place == 0, (d + 15) % 16, d)
    right = jnp.where(place == 15, (d + 1) % 16, d)
    row = lax.broadcasted_iota(jnp.int32, (BS, LANES), 0)

    planes = []
    for ref, index, which in ((before_ref, left, 0), (None, d, 2), (after_ref, right, 1)):
        centre = n_ref[0, 44] if ref is None else ref[0, 0]
        low = low_ref[index, pl.ds(which, 1), :]
        high = high_ref[index, pl.ds(which, 1), :]
        minus = jnp.where(row == 0, low, pltpu.roll(centre, 1, 0))
        plus = jnp.where(row == BS - 1, high, pltpu.roll(centre, BS - 1, 0))
        smooth_y = (2.0 / 3.0) * centre + (1.0 / 6.0) * (minus + plus)
        planes.append((smooth_y, plus - minus))

    def along_z(v):
        return pltpu.roll(v, LANES - 1, 1), pltpu.roll(v, 1, 1)

    def smooth_z(v):
        plus, minus = along_z(v)
        return (2.0 / 3.0) * v + (1.0 / 6.0) * (plus + minus)

    grad_x = 0.5 * smooth_z(planes[2][0] - planes[0][0])
    sides = planes[0][1] + planes[2][1]
    grad_y = 0.5 * smooth_z((2.0 / 3.0) * planes[1][1] + (1.0 / 6.0) * sides)
    sides = planes[0][0] + planes[2][0]
    plus, minus = along_z((2.0 / 3.0) * planes[1][0] + (1.0 / 6.0) * sides)
    grad_z = 0.5 * (plus - minus)
    flag_line = flag_ref[pl.ds(d, 1), :]

    for half in range(2):
        rows = slice(half * 8, half * 8 + 8)
        at = pl.ds(half * 8, 8)
        f = [n_ref[0, q, at, :] for q in range(27)]
        phase = n_ref[0, 44, at, :]
        raw = to_moments(f)
        velocity = (raw[9], raw[3], raw[1])
        rest = equil_moments(raw[0], velocity)
        clipped = jnp.clip(phase, 0.0, 1.0)
        density = 0.001 + 0.999 * clipped
        dynamic = 1e-05 + 0.09999 * clipped
        shear = density / (0.5 * density + 3.0 * dynamic)
        scaled = [0.0] * 27
        for q in range(27):
            fold = 0.5 ** sum(n != 0 for n in (q // 9, q // 3 % 3, q % 3))
            rate = shear if q in (4, 10, 12) else rate_ref[q]
            scaled[q] = (rate * fold) * (raw[q] - rest[q])
        back = from_moments(scaled)

        def put(kind, index, v, value):
            if v[2] != 0:
                value = pltpu.roll(value, v[2] % LANES, 1)
            to = d if v[0] == 0 else (left if v[0] < 0 else right)
            out_ref[to, PLACE[kind, index], at, :] = value

        for q in range(27):
            put("h", q, FULL[q], f[q] - back[q])

        g = (grad_x[rows], grad_y[rows], grad_z[rows])
        scale = lax.rsqrt(g[0] * g[0] + g[1] * g[1] + g[2] * g[2] + 0.25)
        sharp = flag_line * (4.0 * phase * (1.0 - phase)) * scale
        drive = [3.0 * phase * velocity[n] + sharp * g[n] for n in range(3)]
        for k in range(15):
            w = weighted(SMALL[k], SMALL_WEIGHT)
            pop = n_ref[0, 27 + k, at, :]
            push = dot(SMALL[k], drive)
            equil = w * (phase if push is None else phase + push)
            put("p", k, SMALL[k], pop - (pop - equil) * (1.0 / 0.7))


def collide(place, rates, field, low, high, flag_lines):
    whole = pl.BlockSpec(memory_space=pltpu.VMEM)

    def shifted(comp, edge, step):
        return pl.BlockSpec(
            (1, 1, BS, LANES),
            lambda d, i: (jnp.where(i[0] == edge, (d + step) % 16, d), comp, 0, 0),
        )

    return pl.pallas_call(
        collide_kernel,
        grid_spec=pltpu.PrefetchScalarGridSpec(
            num_scalar_prefetch=1,
            grid=(16,),
            in_specs=[
                pl.BlockSpec(memory_space=pltpu.SMEM),
                pl.BlockSpec((1, 45, BS, LANES), lambda d, i: (d, 0, 0, 0)),
                shifted(42, 0, 15),
                shifted(43, 15, 1),
                whole,
                whole,
                whole,
            ],
            out_specs=pl.BlockSpec((16, 42, BS, LANES), lambda d, i: (0, 0, 0, 0)),
        ),
        out_shape=jax.ShapeDtypeStruct((16, 42, BS, LANES), jnp.float32),
        compiler_params=pltpu.CompilerParams(vmem_limit_bytes=VMEM_LIMIT),
    )(place, rates, field, field, field, low, high, flag_lines)


def finish_kernel(minus_ref, zero_ref, plus_ref, low_ref, high_ref, hydro_ref, phase_ref):
    x = pl.program_id(0)
    row = lax.broadcasted_iota(jnp.int32, (BS, LANES), 0)
    for n, (kind, index, v) in enumerate(ORDER):
        source = (minus_ref, zero_ref, plus_ref)[v[0] + 1]
        value = source[0, n % 14]
        at = (x - v[0] + 16) % 16
        if v[1] == 1:
            face = low_ref[at, pl.ds(UP_FACE.index(n), 1), :]
            value = jnp.where(row == 0, face, pltpu.roll(value, 1, 0))
        elif v[1] == -1:
            face = high_ref[at, pl.ds(DOWN_FACE.index(n), 1), :]
            value = jnp.where(row == BS - 1, face, pltpu.roll(value, BS - 1, 0))
        (hydro_ref if kind == "h" else phase_ref)[index, 0] = value


def finish(got, low, high):
    whole = pl.BlockSpec(memory_space=pltpu.VMEM)

    def part(group, step):
        return pl.BlockSpec((1, 14, BS, LANES), lambda x: ((x + step) % 16, group, 0, 0))

    return pl.pallas_call(
        finish_kernel,
        grid=(16,),
        in_specs=[part(0, 1), part(1, 0), part(2, 15), whole, whole],
        out_specs=[
            pl.BlockSpec((27, 1, BS, LANES), lambda x: (0, x, 0, 0)),
            pl.BlockSpec((15, 1, BS, LANES), lambda x: (0, x, 0, 0)),
        ],
        out_shape=[
            jax.ShapeDtypeStruct((27, BS, BS, LANES), jnp.float32),
            jax.ShapeDtypeStruct((15, BS, BS, LANES), jnp.float32),
        ],
        compiler_params=pltpu.CompilerParams(vmem_limit_bytes=VMEM_LIMIT),
    )(got, got, got, low, high)


def swap_faces(upper, lower):
    size = lax.axis_size("gy")
    up = [(i, (i + 1) % size) for i in range(size)]
    down = [(j, i) for i, j in up]
    return lax.ppermute(upper, "gy", up), lax.ppermute(lower, "gy", down)


def on_device(hydro_old, phase_old, targets, flags, relax_rates):
    place = lax.axis_index("gx").astype(jnp.int32).reshape(1)
    slots = targets.shape[1]
    packed, place = pack(place, hydro_old[0], phase_old[0], targets, flags)
    got = lax.all_to_all(packed, "gx", split_axis=0, concat_axis=0, tiled=True)
    label = got[:, slots * SLOT_ROWS, :slots].astype(jnp.int32)
    flag = got[:, slots * SLOT_ROWS + 1, :slots]
    match = label.reshape(1, -1) == jnp.arange(128, dtype=jnp.int32)[:, None]
    order = jnp.arange(16 * slots, dtype=jnp.int32)
    where = jnp.sum(jnp.where(match, order[None, :], 0), axis=1)
    where = jnp.stack([where // slots, where % slots])
    flag_of = jnp.sum(jnp.where(match, flag.reshape(1, -1), 0.0), axis=1)
    flag_lines = jnp.repeat(flag_of.reshape(16, BZ), BS, axis=1)

    field = spread(where, got)
    low, high = swap_faces(field[:, 42:45, BS - 1, :], field[:, 42:45, 0, :])
    send = collide(place, relax_rates, field, low, high, flag_lines)
    final = lax.all_to_all(send, "gx", split_axis=0, concat_axis=0, tiled=True)
    upper = jnp.concatenate([final[:, a:b, BS - 1, :] for a, b in runs(UP_FACE)], axis=1)
    lower = jnp.concatenate([final[:, a:b, 0, :] for a, b in runs(DOWN_FACE)], axis=1)
    low, high = swap_faces(upper, lower)
    return tuple(finish(final, low, high))


def solution(mesh):
    in_specs = (
        P("gy", "gx", None, None),
        P("gy", "gx", None, None),
        P("gy", "gx"),
        P("gy", "gx"),
        P(),
    )
    out_specs = (P(None, "gx", "gy", None), P(None, "gx", "gy", None))
    return jax.shard_map(
        on_device, mesh=mesh, in_specs=in_specs, out_specs=out_specs, check_vma=False
    )
```

time: 620 us -> 225 us (0.36)
  the two profiles are of different devices: /device:TPU:29 before, /device:TPU:1 now
where the time goes in v1:
time: 225 us; the launch traced here: 223 us
  blocking collectives  151 us (67%)
  Pallas kernels  50.8 us (23%)
  waiting for transfers between devices  6.93 us (3%)
  local copies, waits for them, and re-layouts  6.34 us (3%)
  starting transfers between devices  5.29 us (2%)
    all_to_all x1, blocking collectives, on_device(): got = lax.all_to_all(packed, 'gx', split_axis=0, concat_axis=0, tiled=True)  82.9 us
    all_to_all x1, blocking collectives, on_device(): final = lax.all_to_all(send, 'gx', split_axis=0, concat_axis=0, tiled=True)  68.2 us
    pallas_call x1, Pallas kernels, spread(): pl.pallas_call(spread_kernel, grid_spec=pltpu.PrefetchScalarGridSpec(num_...  16.7 us
    pallas_call x1, Pallas kernels, collide(): pl.pallas_call(collide_kernel, grid_spec=pltpu.PrefetchScalarGridSpec(num...  13.6 us
    pallas_call x1, Pallas kernels, finish(): pl.pallas_call(finish_kernel, grid=(16,), in_specs=[part(0, 1), part(1, 0...  11.2 us
    pallas_call x1, Pallas kernels, pack(): pl.pallas_call(pack_kernel, grid=(slots + 1,), in_specs=[pl.BlockSpec(mem...  9.28 us
    ppermute x4, waiting for transfers between devices, swap_faces(): return (lax.ppermute(upper, 'gy', up), lax.ppermute(lower, 'gy', down))  6.93 us
    ppermute x4, starting transfers between devices, swap_faces(): return (lax.ppermute(upper, 'gy', up), lax.ppermute(lower, 'gy', down))  5.29 us
  transfers between devices with their start and end apart: 4, of which 3 were waited for; matrix products, arithmetic and copies ran while one was open for 0% of the time, Pallas kernels for 0%

profile of v1, /device:TPU:1, one launch (start us, length us, event | category | flops | bytes accessed | tf_op | source)
XLA Modules:
  0.0 222.9 jit_solution(5952023437911293469)
XLA Ops:
  0.6 9.3 %shard_map.68 = (f32[16,800,128]{2,1,0:T(8,128)}, s32[1]{0:T(128)}) custom-call(s32[1]{0:T(128)} %bitcast.place_ref, f32[9,27,32,128]{3,2,1,0:T(8,128)} %bitcast.32, f32[9,15,32,128]{3,2,1,0:T(8,128)} %bitcast.33, s32[1,9]{1,0:T(1,128)} %target_ref.1, s32[1,9]{1,0:T(1,128)} %flag_ref.1), custom_call_target="tpu_custom_call" | custom-call | tf_op jit(solution)/shard_map/pallas_call | solution.py:77
  9.9 82.9 %all_to_all.10.refs_0_.refs_1_.refs_2_.refs_3_.refs_4_.refs_5_.refs_6_.refs_7_ = f32[16,800,128]{2,1,0:T(8,128)S(1)} all-to-all(f32[16,800,128]{2,1,0:T(8,128)} %get-tuple-element.5), channel_id=1, replica_groups=mesh['gx'=16,'gy'=8] {'gx'}, dimensions={0} | all-to-all | bytes 13107200 | tf_op jit(solution)/shard_map/all_to_all | solution.py:373
  92.8 0.0 copy-start
  92.8 2.7 %copy-done = f32[16,800,128]{2,1,0:T(8,128)} copy-done((f32[16,800,128]{2,1,0:T(8,128)}, f32[16,800,128]{2,1,0:T(8,128)S(1)}, u32[]{:S(2)}) %copy-start) | copy-done | bytes 6553624
  95.6 0.1 broadcast_in_dim.33
  95.7 0.9 fusion
  96.6 0.1 convert_element_type.11
  96.6 0.1 select_reduce_fusion.1
  96.8 0.6 pad_add_fusion.where_ref
  97.3 16.7 %shard_map.69.n_ref.before_ref.after_ref = f32[16,45,16,128]{3,2,1,0:T(8,128)} custom-call(s32[2,128]{1,0:T(2,128)} %pad_add_fusion.where_ref, f32[16,800,128]{2,1,0:T(8,128)} %copy-done, f32[16,800,128]{2,1,0:T(8,128)} %copy-done, f32[16,800,128]{2,1,0:T(8,128)} %copy-done, f32[16,800,128]{2,1,0:T(8,128)} %copy-done, f32[16,800,128]{2,1,0:T(8,128)} %copy-done, ...), custom_call_target="tpu_custom_call" | custom-call | tf_op jit(solution)/shard_map/pallas_call | solution.py:143
  114.1 1.1 fusion.2
  115.2 3.9 %collective-permute-start = (f32[16,3,128]{2,1,0:T(4,128)S(1)}, f32[16,3,128]{2,1,0:T(4,128)S(1)}, u32[]{:S(2)}, u32[]{:S(2)}) collective-permute-start(f32[16,3,128]{2,1,0:T(4,128)S(1)} %bitcast.37), channel_id=1, source_target_pairs={{0,1},{1,2},{2,3},{3,4},{4,5},{5,6},{6,7},{7,0},{8,9},{9,10},{10,1... | collective-permute-start | bytes 73736 | tf_op jit(solution)/shard_map/ppermute | solution.py:366
  119.0 0.0 collective-permute-start.1
  119.1 0.1 select_reduce_fusion
  119.2 0.1 reshape.73
  119.3 0.1 broadcast_in_dim.36
  119.3 0.7 reshape.74.flag_ref
  120.0 0.0 collective-permute-done.low_ref
  120.1 2.3 %collective-permute-done.1.high_ref = f32[16,3,128]{2,1,0:T(4,128)S(1)} collective-permute-done((f32[16,3,128]{2,1,0:T(4,128)S(1)}, f32[16,3,128]{2,1,0:T(4,128)S(1)}, u32[]{:S(2)}, u32[]{:S(2)}) %collective-permute-start.1) | collective-permute-done | bytes 24608 | tf_op jit(solution)/shard_map/ppermute | solution.py:366
  122.4 0.0 copy-done.4
  122.4 0.6 copy-done.5
  123.0 13.6 %shard_map.70 = f32[16,42,16,128]{3,2,1,0:T(8,128)} custom-call(s32[1]{0:T(128)} %get-tuple-element.4.place_ref, f32[27]{0:T(128)} %rate_ref.1, f32[16,45,16,128]{3,2,1,0:T(8,128)} %shard_map.69.n_ref.before_ref.after_ref, f32[16,45,16,128]{3,2,1,0:T(8,128)} %shard_map.69.n_ref.before_ref.after_ref, ...), custom_call_target="tpu_custom_call" | custom-call | tf_op jit(solution)/shard_map/pallas_call | solution.py:303
  136.7 68.2 %all_to_all.11.minus_ref.zero_ref.plus_ref = f32[16,42,16,128]{3,2,1,0:T(8,128)S(1)} all-to-all(f32[16,42,16,128]{3,2,1,0:T(8,128)} %shard_map.70), channel_id=1, replica_groups=mesh['gx'=16,'gy'=8] {'gx'}, dimensions={0} | all-to-all | bytes 11010048 | tf_op jit(solution)/shard_map/all_to_all | solution.py:386
  204.8 0.1 fusion.3
  205.1 1.3 collective-permute-start.2
  206.4 0.1 collective-permute-start.3
  206.5 1.8 collective-permute-done.2.low_ref
  208.3 2.8 %collective-permute-done.3.high_ref = f32[16,14,128]{2,1,0:T(8,128)S(1)} collective-permute-done((f32[16,14,128]{2,1,0:T(8,128)S(1)}, f32[16,14,128]{2,1,0:T(8,128)S(1)}, u32[]{:S(2)}, u32[]{:S(2)}) %collective-permute-start.3) | collective-permute-done | bytes 114720 | tf_op jit(solution)/shard_map/ppermute | solution.py:366
  211.1 0.0 copy-done.1
  211.1 0.0 copy-done.2
  211.1 0.7 copy-done.3
  211.8 11.2 %shard_map.71 = (f32[27,16,16,128]{3,2,1,0:T(8,128)}, f32[15,16,16,128]{3,2,1,0:T(8,128)}) custom-call(f32[16,42,16,128]{3,2,1,0:T(8,128)} %copy-done.1, f32[16,42,16,128]{3,2,1,0:T(8,128)} %copy-done.1, f32[16,42,16,128]{3,2,1,0:T(8,128)} %copy-done.1, f32[16,14,128]{2,1,0:T(8,128)} %copy-done.2, f32[16,14,128]{2,1,0:T(8,128)} %copy-done.3), custom_call_target="tpu_custom_call" | custom-call | tf_op jit(solution)/shard_map/pallas_call | solution.py:346
  (14 shorter events, 0.2 us)
Async XLA Ops:
  92.8 2.7 %copy-start = (f32[16,800,128]{2,1,0:T(8,128)}, f32[16,800,128]{2,1,0:T(8,128)S(1)}, u32[]{:S(2)}) copy-start(f32[16,800,128]{2,1,0:T(8,128)S(1)} %all_to_all.10.refs_0_.refs_1_.refs_2_.refs_3_.refs_4_.refs_5_.refs_6_.refs_7_) | copy-start | bytes 19660804
  115.2 4.9 %collective-permute-start = (f32[16,3,128]{2,1,0:T(4,128)S(1)}, f32[16,3,128]{2,1,0:T(4,128)S(1)}, u32[]{:S(2)}, u32[]{:S(2)}) collective-permute-start(f32[16,3,128]{2,1,0:T(4,128)S(1)} %bitcast.37), channel_id=1, source_target_pairs={{0,1},{1,2},{2,3},{3,4},{4,5},{5,6},{6,7},{7,0},{8,9},{9,10},{10,1... | collective-permute-start | bytes 73736 | tf_op jit(solution)/shard_map/ppermute | solution.py:366
  119.0 3.3 %collective-permute-start.1 = (f32[16,3,128]{2,1,0:T(4,128)S(1)}, f32[16,3,128]{2,1,0:T(4,128)S(1)}, u32[]{:S(2)}, u32[]{:S(2)}) collective-permute-start(f32[16,3,128]{2,1,0:T(4,128)S(1)} %bitcast.36), channel_id=1, source_target_pairs={{1,0},{2,1},{3,2},{4,3},{5,4},{6,5},{7,6},{0,7},{9,8},{10,9},{11,1... | collective-permute-start | bytes 73736 | tf_op jit(solution)/shard_map/ppermute | solution.py:366
  120.1 2.3 %copy-start.4 = (f32[16,3,128]{2,1,0:T(4,128)}, f32[16,3,128]{2,1,0:T(4,128)S(1)}, u32[]{:S(2)}) copy-start(f32[16,3,128]{2,1,0:T(4,128)S(1)} %collective-permute-done.low_ref) | copy-start | bytes 73732
  122.4 0.6 copy-start.5
  204.8 6.3 %copy-start.1 = (f32[16,42,16,128]{3,2,1,0:T(8,128)}, f32[16,42,16,128]{3,2,1,0:T(8,128)S(1)}, u32[]{:S(2)}) copy-start(f32[16,42,16,128]{3,2,1,0:T(8,128)S(1)} %all_to_all.11.minus_ref.zero_ref.plus_ref) | copy-start | bytes 16515076
  205.1 3.2 %collective-permute-start.2 = (f32[16,14,128]{2,1,0:T(8,128)S(1)}, f32[16,14,128]{2,1,0:T(8,128)S(1)}, u32[]{:S(2)}, u32[]{:S(2)}) collective-permute-start(f32[16,14,128]{2,1,0:T(8,128)S(1)} %pad_maximum_fusion), channel_id=1, source_target_pairs={{0,1},{1,2},{2,3},{3,4},{4,5},{5,6},{6,7},{7,0},{8,9},{9,10},{10,1... | collective-permute-start | bytes 344072 | tf_op jit(solution)/shard_map/ppermute | solution.py:366
  206.4 4.7 %collective-permute-start.3 = (f32[16,14,128]{2,1,0:T(8,128)S(1)}, f32[16,14,128]{2,1,0:T(8,128)S(1)}, u32[]{:S(2)}, u32[]{:S(2)}) collective-permute-start(f32[16,14,128]{2,1,0:T(8,128)S(1)} %pad_maximum_fusion.1), channel_id=1, source_target_pairs={{1,0},{2,1},{3,2},{4,3},{5,4},{6,5},{7,6},{0,7},{9,8},{10,9},{11,1... | collective-permute-start | bytes 344072 | tf_op jit(solution)/shard_map/ppermute | solution.py:366
  208.3 2.8 %copy-start.2 = (f32[16,14,128]{2,1,0:T(8,128)}, f32[16,14,128]{2,1,0:T(8,128)S(1)}, u32[]{:S(2)}) copy-start(f32[16,14,128]{2,1,0:T(8,128)S(1)} %collective-permute-done.2.low_ref) | copy-start | bytes 344068
  211.1 0.7 copy-start.3

commit v2 on v1

v2 whole, which is shorter than its diff:
```python
import functools

import jax
import jax.numpy as jnp
import numpy as np
from jax import lax
from jax.experimental import pallas as pl
from jax.experimental.pallas import tpu as pltpu
from jax.sharding import PartitionSpec as P

BS = 16
BZ = 8
SLOT_ROWS = 88
AHEAD = 4
LANES = 128
MIB = 1024 * 1024
ANY = pl.BlockSpec(memory_space=pl.ANY)
SMEM = pl.BlockSpec(memory_space=pltpu.SMEM)
WHOLE = pl.BlockSpec(memory_space=pltpu.VMEM)


def room(mib):
    return pltpu.CompilerParams(vmem_limit_bytes=mib * MIB)


def buffer(*shape):
    return pltpu.VMEM(shape, jnp.float32)


def made(*shape):
    return jax.ShapeDtypeStruct(shape, jnp.float32)

FULL = [(a, b, c) for a in (-1, 0, 1) for b in (-1, 0, 1) for c in (-1, 0, 1)]
SMALL = [v for v in FULL if sum(map(abs, v)) != 2]
ORDER = sorted(
    [("h", q, v) for q, v in enumerate(FULL)] + [("p", k, v) for k, v in enumerate(SMALL)],
    key=lambda t: (t[2][0], t[0], t[2][1] if t[0] == "h" else -t[2][1], t[1]),
)
PLACE = {(kind, index): n for n, (kind, index, _) in enumerate(ORDER)}
UP_FACE = [n for n, t in enumerate(ORDER) if t[2][1] == 1]
DOWN_FACE = [n for n, t in enumerate(ORDER) if t[2][1] == -1]


def runs(places):
    out = []
    for n in places:
        if out and out[-1][1] == n:
            out[-1][1] = n + 1
        else:
            out.append([n, n + 1])
    return out


def pack_kernel(
    place_ref, h_in, p_in, target_ref, flag_ref, out, here_ref, h_ref, p_ref, o_ref, tag_ref, h_sem, p_sem, o_sem, tag_sem
):
    slots = target_ref.shape[1]
    here_ref[0] = place_ref[0]

    def load(s):
        return (
            pltpu.make_async_copy(h_in.at[s], h_ref.at[s], h_sem.at[s]),
            pltpu.make_async_copy(p_in.at[s], p_ref.at[s], p_sem.at[s]),
        )

    def leave(s):
        rows = pl.ds(pl.multiple_of(s * SLOT_ROWS, 8), SLOT_ROWS)
        return pltpu.make_async_copy(o_ref.at[s], out.at[:, rows, :], o_sem.at[s])

    for s in range(slots):
        for copy in load(s):
            copy.start()
    tag_ref[:, 0:1, 0:slots] = jnp.broadcast_to(target_ref[...].astype(jnp.float32), (BS, 1, slots))
    tag_ref[:, 1:2, 0:slots] = jnp.broadcast_to(flag_ref[...].astype(jnp.float32), (BS, 1, slots))
    tags = pltpu.make_async_copy(tag_ref, out.at[:, pl.ds(slots * SLOT_ROWS, 8), :], tag_sem)
    tags.start()

    @pl.loop(0, slots)
    def _(s):
        for copy in load(s):
            copy.wait()
        totals = [sum(p_ref[s, k, pl.ds(part * 8, 8), :] for k in range(15)) for part in range(4)]
        for part in range(4):
            rows = pl.ds(part * 8, 8)
            groups = [[h_ref[s, 4 * n + m, rows, :] for m in range(4)] for n in range(6)]
            groups += [[p_ref[s, 4 * n + m, rows, :] for m in range(4)] for n in range(3)]
            last_h = [h_ref[s, 24 + m, rows, :] for m in range(3)]
            last_p = [p_ref[s, 12 + m, rows, :] for m in range(3)]
            groups += [last_p + [beside(totals, part, -1)], last_h + [beside(totals, part, 1)]]
            for n, group in enumerate(groups):
                for m, value in enumerate(swap_bits(group, 0, 2)):
                    o_ref[s, part * 4 + m, pl.ds(n * 8, 8), :] = value
        leave(s).start()

    for s in range(slots):
        leave(s).wait()
    tags.wait()


def beside(totals, part, side):
    near, far = totals[part], totals[(part + side) % 4]
    row = lax.broadcasted_iota(jnp.int32, (8, LANES), 0)
    if side < 0:
        return jnp.where(row < 2, pltpu.roll(far, 2, 0), pltpu.roll(near, 2, 0))
    return jnp.where(row >= 6, pltpu.roll(far, 6, 0), pltpu.roll(near, 6, 0))


def pack(place, hydro, phase, targets, flags):
    slots = hydro.shape[0]
    return pl.pallas_call(
        pack_kernel,
        in_specs=[SMEM, ANY, ANY, WHOLE, WHOLE],
        out_specs=[ANY, SMEM],
        out_shape=[
            made(BS, slots * SLOT_ROWS + 8, LANES),
            jax.ShapeDtypeStruct((1,), jnp.int32),
        ],
        scratch_shapes=[
            buffer(slots, 27, 32, LANES),
            buffer(slots, 15, 32, LANES),
            buffer(slots, BS, SLOT_ROWS, LANES),
            buffer(BS, 8, LANES),
            pltpu.SemaphoreType.DMA((slots,)),
            pltpu.SemaphoreType.DMA((slots,)),
            pltpu.SemaphoreType.DMA((slots,)),
            pltpu.SemaphoreType.DMA,
        ],
        compiler_params=room(60),
    )(place, hydro.reshape(slots, 27, 32, LANES), phase.reshape(slots, 15, 32, LANES), targets, flags)


def swap_bits(values, axis, unit):
    count = len(values)
    size = count * unit
    position = lax.broadcasted_iota(jnp.int32, (8, LANES), axis) // unit
    step = 1
    while step < count:
        high = (position & step) != 0
        fresh = list(values)
        for n in range(count):
            if n & step:
                continue
            a, b = values[n], values[n + step]
            fresh[n] = jnp.where(high, pltpu.roll(b, step * unit, axis), a)
            fresh[n + step] = jnp.where(high, b, pltpu.roll(a, size - step * unit, axis))
        values = fresh
        step *= 2
    return values


def swap_lanes(values):
    position = lax.broadcasted_iota(jnp.int32, (8, LANES), 1) // 16

    def skew(parts):
        for step in (1, 2, 4):
            high = (position & step) != 0
            parts = [jnp.where(high, parts[(n - step) % 8], parts[n]) for n in range(8)]
        return parts

    parts = skew([values[-n % 8] for n in range(8)])
    return skew([parts[0]] + [pltpu.roll(parts[n], LANES - 16 * n, 1) for n in range(1, 8)])


GROUPS = [[4 * n + m for m in range(4)] for n in range(6)]
GROUPS += [[27 + 4 * n + m for m in range(4)] for n in range(3)]
GROUPS += [[39, 40, 41, 42], [24, 25, 26, 43]]


def survey_kernel(got, code_ref, sum_ref, up_ref, down_ref, tag_ref, b_ref, code_s, tag_sem, b_sem, code_sem):
    slots = b_ref.shape[0]
    tags = pltpu.make_async_copy(got.at[:, pl.ds(slots * SLOT_ROWS, 8), :], tag_ref, tag_sem)
    tags.start()
    loads = [
        pltpu.make_async_copy(got.at[:, pl.ds(t * SLOT_ROWS + 48, 40), :], b_ref.at[t], b_sem.at[t])
        for t in range(slots)
    ]
    for copy in loads:
        copy.start()
    tags.wait()

    row = lax.broadcasted_iota(jnp.int32, (8, LANES), 0)
    value = lax.broadcasted_iota(jnp.int32, (8, LANES), 1).astype(jnp.float32)
    code = jnp.zeros((8, LANES), jnp.float32)
    for half in range(2):
        label = tag_ref[pl.ds(half * 8, 8), 0, :]
        flag = tag_ref[pl.ds(half * 8, 8), 1, :]
        sender = ((row + half * 8) * 32).astype(jnp.float32)
        for t in range(slots):
            match = jnp.broadcast_to(label[:, t : t + 1], (8, LANES)) == value
            entry = sender + (2.0 * t + jnp.broadcast_to(flag[:, t : t + 1], (8, LANES)))
            code = code + jnp.where(match, entry, 0.0)
    code_ref[...] = jnp.sum(code, axis=0, keepdims=True).astype(jnp.int32)
    table = pltpu.make_async_copy(code_ref, code_s, code_sem)
    table.start()
    table.wait()
    for copy in loads:
        copy.wait()

    @pl.loop(0, 16)
    def _(d):
        values = []
        for level in range(8):
            sender, slot, _ = decode(code_s[0, d * 8 + level])
            parts = [b_ref[slot, sender, pl.ds(n * 8, 8), :] for n in range(5)]
            own = parts[0] + parts[1] + parts[2] + jnp.where(row < 6, parts[3], 0.0)
            own = own + pltpu.roll(own, 2, 0)
            own = own + pltpu.roll(own, 4, 0)
            beyond = jnp.where(row < 4, pltpu.roll(parts[4], 4, 0), own)
            values.append(jnp.where(row < 2, pltpu.roll(parts[3], 2, 0), beyond))
        values = swap_bits(swap_lanes(values), 0, 1)
        for n in range(6):
            sum_ref[d, n // 2, pl.ds((n % 2) * 8, 8), :] = values[n]
        up_ref[d] = sum_ref[d, :, BS - 1, :]
        down_ref[d] = sum_ref[d, :, 0, :]


def decode(code):
    return lax.shift_right_logical(code, 5), lax.shift_right_logical(code, 1) & 15, code & 1


def survey(got, slots):
    return pl.pallas_call(
        survey_kernel,
        in_specs=[ANY],
        out_specs=[WHOLE, WHOLE, WHOLE, WHOLE],
        out_shape=[
            jax.ShapeDtypeStruct((1, LANES), jnp.int32),
            made(16, 3, BS, LANES),
            made(16, 3, LANES),
            made(16, 3, LANES),
        ],
        scratch_shapes=[
            buffer(16, 8, LANES),
            buffer(slots, 16, 40, LANES),
            pltpu.SMEM((1, LANES), jnp.int32),
            pltpu.SemaphoreType.DMA,
            pltpu.SemaphoreType.DMA((slots,)),
            pltpu.SemaphoreType.DMA,
        ],
        compiler_params=room(60),
    )(got)


def to_moments(f):
    f = list(f)
    for stride in (1, 3, 9):
        for n in range(27):
            if (n // stride) % 3 == 0:
                low, mid, high = f[n], f[n + stride], f[n + 2 * stride]
                both = low + high
                f[n], f[n + stride], f[n + 2 * stride] = both + mid, high - low, both
    return f


def from_moments(m):
    m = list(m)
    for stride in (1, 3, 9):
        for n in range(27):
            if (n // stride) % 3 == 0:
                zero, one, two = m[n], m[n + stride], m[n + 2 * stride]
                low, high = two - one, two + one
                m[n], m[n + stride], m[n + 2 * stride] = low, zero - (low + high), high
    return m


def equil_moments(pressure, velocity):
    x, y, z = velocity
    squares = (x * x, y * y, z * z)
    cross = {(1, 1, 0): x * y, (1, 0, 1): x * z, (0, 1, 1): y * z}
    third = pressure * (1.0 / 3.0)
    total = squares[0] + squares[1] + squares[2]
    out = [None] * 27
    for q in range(27):
        powers = (q // 9, q // 3 % 3, q % 3)
        ones = tuple(int(n == 1) for n in powers)
        scale = (1.0 / 3.0) ** sum(n == 2 for n in powers)
        if sum(ones) == 0:
            two = [squares[n] for n in range(3) if powers[n] == 2]
            value = pressure if not two else pressure + 3.0 * sum(two[1:], two[0])
            out[q] = value if scale == 1.0 else scale * value
        elif sum(ones) == 1:
            value = velocity[ones.index(1)]
            out[q] = value if scale == 1.0 else scale * value
        elif sum(ones) == 2:
            out[q] = cross[ones] if scale == 1.0 else scale * cross[ones]
        else:
            out[q] = 0.0
    return out


def weighted(v, table):
    return table[sum(map(abs, v))]


FULL_WEIGHT = [8.0 / 27.0, 2.0 / 27.0, 1.0 / 54.0, 1.0 / 216.0]
SMALL_WEIGHT = [2.0 / 9.0, 1.0 / 9.0, 0.0, 1.0 / 72.0]


def dot(v, parts):
    total = None
    for c, part in zip(v, parts):
        if c != 0:
            if total is None:
                total = part if c > 0 else -part
            else:
                total = total + part if c > 0 else total - part
    return total


def collide_kernel(
    place_ref, rate_ref, code_ref, got, sums, low, high, out,
    sum_ref, low_ref, high_ref, b_ref, n_ref, o_ref, side_sem, b_sem, o_sem,
):
    place = place_ref[0]
    sides = [
        pltpu.make_async_copy(a, b, side_sem.at[n])
        for n, (a, b) in enumerate(((sums, sum_ref), (low, low_ref), (high, high_ref)))
    ]

    def start(d):
        for level in range(8):
            sender, slot, _ = decode(code_ref[0, d * 8 + level])
            rows = pl.ds(pl.multiple_of(slot * SLOT_ROWS, 8), SLOT_ROWS)
            pltpu.make_async_copy(got.at[sender, rows, :], b_ref.at[d, level], b_sem.at[d]).start()

    def leave(d):
        left = jnp.where(place == 0, (d + 15) % 16, d)
        right = jnp.where(place == 15, (d + 1) % 16, d)
        for group, to in enumerate((left, d, right)):
            comps = pl.ds(group * 14, 14)
            yield pltpu.make_async_copy(o_ref.at[d, comps], out.at[to, comps], o_sem.at[d, group])

    for copy in sides:
        copy.start()
    for d in range(AHEAD):
        start(d)
    for copy in sides:
        copy.wait()

    @pl.loop(0, 16)
    def _(d):
        @pl.when(d + AHEAD < 16)
        def _():
            start(d + AHEAD)

        pltpu.make_async_copy(b_ref.at[d], b_ref.at[d], b_sem.at[d]).wait()
        for group, comps in enumerate(GROUPS):
            values = [b_ref[d, level, pl.ds(group * 8, 8), :] for level in range(8)]
            values = swap_bits(swap_lanes(values), 0, 1)
            for n in range(8):
                if comps[n // 2] < 42:
                    n_ref[comps[n // 2], pl.ds((n % 2) * 8, 8), :] = values[n]
        position = lax.broadcasted_iota(jnp.int32, (8, LANES), 1) // 16
        flag_line = jnp.zeros((8, LANES), jnp.float32)
        for level in range(8):
            flag = decode(code_ref[0, d * 8 + level])[2].astype(jnp.float32)
            flag_line = jnp.where(position == level, flag, flag_line)
        collide_plane(d, place, rate_ref, n_ref, sum_ref, low_ref, high_ref, flag_line, o_ref)
        for copy in leave(d):
            copy.start()

    for d in range(16):
        for copy in leave(d):
            copy.wait()


def collide_plane(d, place, rate_ref, n_ref, sum_ref, low_ref, high_ref, flag_line, out_ref):
    left = jnp.where(place == 0, (d + 15) % 16, d)
    right = jnp.where(place == 15, (d + 1) % 16, d)
    row = lax.broadcasted_iota(jnp.int32, (BS, LANES), 0)

    planes = []
    for index, which in ((left, 0), (d, 2), (right, 1)):
        centre = sum_ref[index, which]
        low = low_ref[index, pl.ds(which, 1), :]
        high = high_ref[index, pl.ds(which, 1), :]
        minus = jnp.where(row == 0, low, pltpu.roll(centre, 1, 0))
        plus = jnp.where(row == BS - 1, high, pltpu.roll(centre, BS - 1, 0))
        smooth_y = (2.0 / 3.0) * centre + (1.0 / 6.0) * (minus + plus)
        planes.append((smooth_y, plus - minus))

    def along_z(v):
        return pltpu.roll(v, LANES - 1, 1), pltpu.roll(v, 1, 1)

    def smooth_z(v):
        plus, minus = along_z(v)
        return (2.0 / 3.0) * v + (1.0 / 6.0) * (plus + minus)

    grad_x = 0.5 * smooth_z(planes[2][0] - planes[0][0])
    sides = planes[0][1] + planes[2][1]
    grad_y = 0.5 * smooth_z((2.0 / 3.0) * planes[1][1] + (1.0 / 6.0) * sides)
    sides = planes[0][0] + planes[2][0]
    plus, minus = along_z((2.0 / 3.0) * planes[1][0] + (1.0 / 6.0) * sides)
    grad_z = 0.5 * (plus - minus)

    for half in range(2):
        rows = slice(half * 8, half * 8 + 8)
        at = pl.ds(half * 8, 8)
        f = [n_ref[q, at, :] for q in range(27)]
        phase = sum_ref[d, 2, at, :]
        raw = to_moments(f)
        velocity = (raw[9], raw[3], raw[1])
        rest = equil_moments(raw[0], velocity)
        clipped = jnp.clip(phase, 0.0, 1.0)
        density = 0.001 + 0.999 * clipped
        dynamic = 1e-05 + 0.09999 * clipped
        shear = density / (0.5 * density + 3.0 * dynamic)
        scaled = [0.0] * 27
        for q in range(27):
            fold = 0.5 ** sum(n != 0 for n in (q // 9, q // 3 % 3, q % 3))
            rate = shear if q in (4, 10, 12) else rate_ref[q]
            scaled[q] = (rate * fold) * (raw[q] - rest[q])
        back = from_moments(scaled)

        def put(kind, index, v, value):
            if v[2] != 0:
                value = pltpu.roll(value, v[2] % LANES, 1)
            out_ref[d, PLACE[kind, index], at, :] = value

        for q in range(27):
            put("h", q, FULL[q], f[q] - back[q])

        g = (grad_x[rows], grad_y[rows], grad_z[rows])
        scale = lax.rsqrt(g[0] * g[0] + g[1] * g[1] + g[2] * g[2] + 0.25)
        sharp = flag_line * (4.0 * phase * (1.0 - phase)) * scale
        drive = [3.0 * phase * velocity[n] + sharp * g[n] for n in range(3)]
        for k in range(15):
            w = weighted(SMALL[k], SMALL_WEIGHT)
            pop = n_ref[27 + k, at, :]
            push = dot(SMALL[k], drive)
            equil = w * (phase if push is None else phase + push)
            put("p", k, SMALL[k], pop - (pop - equil) * (1.0 / 0.7))


def collide(place, rates, code, got, sums, low, high):
    return pl.pallas_call(
        collide_kernel,
        in_specs=[SMEM, SMEM, SMEM, ANY, ANY, ANY, ANY],
        out_specs=ANY,
        out_shape=made(16, 42, BS, LANES),
        scratch_shapes=[
            buffer(16, 3, BS, LANES),
            buffer(16, 3, LANES),
            buffer(16, 3, LANES),
            buffer(16, 8, SLOT_ROWS, LANES),
            buffer(42, BS, LANES),
            buffer(16, 42, BS, LANES),
            pltpu.SemaphoreType.DMA((3,)),
            pltpu.SemaphoreType.DMA((16,)),
            pltpu.SemaphoreType.DMA((16, 3)),
        ],
        compiler_params=room(60),
    )(place, rates, code, got, sums, low, high)


def finish_kernel(got, low_ref, high_ref, hydro, phase, n_ref, h_ref, p_ref, n_sem, h_sem, p_sem):
    row = lax.broadcasted_iota(jnp.int32, (BS, LANES), 0)

    def load(i):
        return pltpu.make_async_copy(got.at[i], n_ref.at[i], n_sem.at[i])

    def leave(i):
        for group in range(3):
            x = (i + group + 15) % 16
            comps = pl.ds(group * 9, 9)
            yield pltpu.make_async_copy(h_ref.at[i, comps], hydro.at[comps, x], h_sem.at[i, group])
            comps = pl.ds(group * 5, 5)
            yield pltpu.make_async_copy(p_ref.at[i, comps], phase.at[comps, x], p_sem.at[i, group])

    for i in range(16):
        load(i).start()

    @pl.loop(0, 16)
    def _(i):
        load(i).wait()
        for n, (kind, index, v) in enumerate(ORDER):
            value = n_ref[i, n]
            if v[1] == 1:
                face = low_ref[i, pl.ds(UP_FACE.index(n), 1), :]
                value = jnp.where(row == 0, face, pltpu.roll(value, 1, 0))
            elif v[1] == -1:
                face = high_ref[i, pl.ds(DOWN_FACE.index(n), 1), :]
                value = jnp.where(row == BS - 1, face, pltpu.roll(value, BS - 1, 0))
            (h_ref if kind == "h" else p_ref)[i, index] = value
        for copy in leave(i):
            copy.start()

    for i in range(16):
        for copy in leave(i):
            copy.wait()


def finish(got, low, high):
    return pl.pallas_call(
        finish_kernel,
        in_specs=[ANY, WHOLE, WHOLE],
        out_specs=[ANY, ANY],
        out_shape=[made(27, BS, BS, LANES), made(15, BS, BS, LANES)],
        scratch_shapes=[
            buffer(16, 42, BS, LANES),
            buffer(16, 27, BS, LANES),
            buffer(16, 15, BS, LANES),
            pltpu.SemaphoreType.DMA((16,)),
            pltpu.SemaphoreType.DMA((16, 3)),
            pltpu.SemaphoreType.DMA((16, 3)),
        ],
        compiler_params=room(24),
    )(got, low, high)


def swap_faces(upper, lower):
    size = lax.axis_size("gy")
    up = [(i, (i + 1) % size) for i in range(size)]
    down = [(j, i) for i, j in up]
    return lax.ppermute(upper, "gy", up), lax.ppermute(lower, "gy", down)


def on_device(hydro_old, phase_old, targets, flags, relax_rates):
    place = lax.axis_index("gx").astype(jnp.int32).reshape(1)
    slots = targets.shape[1]
    packed, place = pack(place, hydro_old[0], phase_old[0], targets, flags)
    got = lax.all_to_all(packed, "gx", split_axis=0, concat_axis=0, tiled=True)
    code, sums, up, down = survey(got, slots)
    low, high = swap_faces(up, down)
    send = collide(place, relax_rates, code, got, sums, low, high)
    final = lax.all_to_all(send, "gx", split_axis=0, concat_axis=0, tiled=True)
    upper = jnp.concatenate([final[:, a:b, BS - 1, :] for a, b in runs(UP_FACE)], axis=1)
    lower = jnp.concatenate([final[:, a:b, 0, :] for a, b in runs(DOWN_FACE)], axis=1)
    low, high = swap_faces(upper, lower)
    return tuple(finish(final, low, high))


def solution(mesh):
    in_specs = (
        P("gy", "gx", None, None),
        P("gy", "gx", None, None),
        P("gy", "gx"),
        P("gy", "gx"),
        P(),
    )
    out_specs = (P(None, "gx", "gy", None), P(None, "gx", "gy", None))
    return jax.shard_map(
        on_device, mesh=mesh, in_specs=in_specs, out_specs=out_specs, check_vma=False
    )
```

time: 225 us -> 195 us (0.87)
  Pallas kernels: 50.8 us -> 28.7 us
  local copies, waits for them, and re-layouts: 6.34 us -> 0.8 us
    pallas_call x4, Pallas kernels: 50.8 us -> 28.7 us  [the longest x1 11 us: collide(): pl.pallas_call(collide_kernel, in_specs=[SMEM, SMEM, SMEM, ANY, ANY, ANY,...]
    unnamed x14 -> x6, local copies, waits for them, and re-layouts: 4.03 us -> 0.62 us
  transfers between devices with their start and end apart: 4 -> 4, of which waited for: 3 -> 4; matrix products, arithmetic and copies ran while one was open for 0% -> 0% of each run, Pallas kernels for 0% -> 0%
where the time goes in v2:
time: 195 us
  blocking collectives  151 us (77%)
  Pallas kernels  28.7 us (15%)
  waiting for transfers between devices  7.98 us (4%)
  starting transfers between devices  5.26 us (3%)
    all_to_all x1, blocking collectives, on_device(): got = lax.all_to_all(packed, 'gx', split_axis=0, concat_axis=0, tiled=True)  83 us
    all_to_all x1, blocking collectives, on_device(): final = lax.all_to_all(send, 'gx', split_axis=0, concat_axis=0, tiled=True)  68 us
    pallas_call x1, Pallas kernels, collide(): pl.pallas_call(collide_kernel, in_specs=[SMEM, SMEM, SMEM, ANY, ANY, ANY,...  11 us
    ppermute x4, waiting for transfers between devices, swap_faces(): return (lax.ppermute(upper, 'gy', up), lax.ppermute(lower, 'gy', down))  7.98 us
    pallas_call x1, Pallas kernels, pack(): pl.pallas_call(pack_kernel, in_specs=[SMEM, ANY, ANY, WHOLE, WHOLE], out_...  6.92 us
    pallas_call x1, Pallas kernels, survey(): pl.pallas_call(survey_kernel, in_specs=[ANY], out_specs=[WHOLE, WHOLE, WH...  5.39 us
    pallas_call x1, Pallas kernels, finish(): pl.pallas_call(finish_kernel, in_specs=[ANY, WHOLE, WHOLE], out_specs=[AN...  5.36 us
    ppermute x4, starting transfers between devices, swap_faces(): return (lax.ppermute(upper, 'gy', up), lax.ppermute(lower, 'gy', down))  5.26 us
  transfers between devices with their start and end apart: 4, of which 4 were waited for; matrix products, arithmetic and copies ran while one was open for 0% of the time, Pallas kernels for 0%

profile of v2, /device:TPU:1, one launch (start us, length us, event | category | flops | bytes accessed | tf_op | source)
XLA Modules:
  0.0 194.6 jit_solution(5701519367529101470)
XLA Ops:
  0.6 6.9 %shard_map.68 = (f32[16,800,128]{2,1,0:T(8,128)}, s32[1]{0:T(128)}) custom-call(s32[1]{0:T(128)} %bitcast.place_ref, f32[9,27,32,128]{3,2,1,0:T(8,128)} %bitcast.22, f32[9,15,32,128]{3,2,1,0:T(8,128)} %bitcast.23, s32[1,9]{1,0:T(1,128)} %target_ref.1, s32[1,9]{1,0:T(1,128)} %flag_ref.1), custom_call_target="tpu_custom_call" | custom-call | tf_op jit(solution)/shard_map/pallas_call | solution.py:110
  7.6 83.0 %all_to_all.10.got = f32[16,800,128]{2,1,0:T(8,128)} all-to-all(f32[16,800,128]{2,1,0:T(8,128)} %get-tuple-element.9), channel_id=1, replica_groups=mesh['gx'=16,'gy'=8] {'gx'}, dimensions={0} | all-to-all | bytes 13107200 | tf_op jit(solution)/shard_map/all_to_all | solution.py:522
  90.6 5.4 %shard_map.69 = (s32[1,128]{1,0:T(1,128)}, f32[16,3,16,128]{3,2,1,0:T(8,128)}, f32[16,3,128]{2,1,0:T(4,128)}, f32[16,3,128]{2,1,0:T(4,128)}) custom-call(f32[16,800,128]{2,1,0:T(8,128)} %all_to_all.10.got), custom_call_target="tpu_custom_call" | custom-call | tf_op jit(solution)/shard_map/pallas_call | solution.py:222
  96.0 3.9 %collective-permute-start = (f32[16,3,128]{2,1,0:T(4,128)}, f32[16,3,128]{2,1,0:T(4,128)S(1)}, u32[]{:S(2)}, u32[]{:S(2)}) collective-permute-start(f32[16,3,128]{2,1,0:T(4,128)} %get-tuple-element.12), channel_id=1, source_target_pairs={{0,1},{1,2},{2,3},{3,4},{4,5},{5,6},{6,7},{7,0},{8,9},{9,10},{10,1... | collective-permute-start | bytes 73736 | tf_op jit(solution)/shard_map/ppermute | solution.py:515
  99.9 0.0 collective-permute-start.1
  99.9 1.3 collective-permute-done.low
  101.2 0.0 copy-start
  101.2 2.2 %collective-permute-done.1.high = f32[16,3,128]{2,1,0:T(4,128)S(1)} collective-permute-done((f32[16,3,128]{2,1,0:T(4,128)}, f32[16,3,128]{2,1,0:T(4,128)S(1)}, u32[]{:S(2)}, u32[]{:S(2)}) %collective-permute-start.1) | collective-permute-done | bytes 24608 | tf_op jit(solution)/shard_map/ppermute | solution.py:515
  103.4 0.0 copy-start.1
  103.4 0.0 copy-done
  103.4 0.6 copy-done.1
  104.0 11.0 %shard_map.70 = f32[16,42,16,128]{3,2,1,0:T(8,128)} custom-call(s32[1]{0:T(128)} %get-tuple-element.8.place_ref, f32[27]{0:T(128)} %rate_ref.1, s32[1,128]{1,0:T(1,128)} %get-tuple-element.10.code_ref, f32[16,800,128]{2,1,0:T(8,128)} %all_to_all.10.got, f32[16,3,16,128]{3,2,1,0:T(8,128)} %get-tuple-element.11.sums, f32[16,3,128]{2,1,0:T(4,128)} %copy-done, ...), custom_call_target="tpu_custom_call" | custom-call | tf_op jit(solution)/shard_map/pallas_call | solution.py:436
  115.0 68.0 %all_to_all.11.got = f32[16,42,16,128]{3,2,1,0:T(8,128)S(1)} all-to-all(f32[16,42,16,128]{3,2,1,0:T(8,128)} %shard_map.70), channel_id=1, replica_groups=mesh['gx'=16,'gy'=8] {'gx'}, dimensions={0} | all-to-all | bytes 11010048 | tf_op jit(solution)/shard_map/all_to_all | solution.py:526
  183.1 0.1 fusion
  183.3 1.1 collective-permute-start.2
  184.5 0.3 collective-permute-start.3
  184.8 1.6 collective-permute-done.2.low_ref
  186.4 2.8 %collective-permute-done.3.high_ref = f32[16,14,128]{2,1,0:T(8,128)S(1)} collective-permute-done((f32[16,14,128]{2,1,0:T(8,128)S(1)}, f32[16,14,128]{2,1,0:T(8,128)S(1)}, u32[]{:S(2)}, u32[]{:S(2)}) %collective-permute-start.3) | collective-permute-done | bytes 114720 | tf_op jit(solution)/shard_map/ppermute | solution.py:515
  189.2 5.4 %shard_map.71 = (f32[27,16,16,128]{3,2,1,0:T(8,128)}, f32[15,16,16,128]{3,2,1,0:T(8,128)}) custom-call(f32[16,42,16,128]{3,2,1,0:T(8,128)S(1)} %all_to_all.11.got, f32[16,14,128]{2,1,0:T(8,128)S(1)} %collective-permute-done.2.low_ref, f32[16,14,128]{2,1,0:T(8,128)S(1)} %collective-permute-done.3.high_ref), custom_call_target="tpu_custom_call" | custom-call | tf_op jit(solution)/shard_map/pallas_call | solution.py:494
  (8 shorter events, 0.2 us)
Async XLA Ops:
  96.0 5.2 %collective-permute-start = (f32[16,3,128]{2,1,0:T(4,128)}, f32[16,3,128]{2,1,0:T(4,128)S(1)}, u32[]{:S(2)}, u32[]{:S(2)}) collective-permute-start(f32[16,3,128]{2,1,0:T(4,128)} %get-tuple-element.12), channel_id=1, source_target_pairs={{0,1},{1,2},{2,3},{3,4},{4,5},{5,6},{6,7},{7,0},{8,9},{9,10},{10,1... | collective-permute-start | bytes 73736 | tf_op jit(solution)/shard_map/ppermute | solution.py:515
  99.9 3.6 %collective-permute-start.1 = (f32[16,3,128]{2,1,0:T(4,128)}, f32[16,3,128]{2,1,0:T(4,128)S(1)}, u32[]{:S(2)}, u32[]{:S(2)}) collective-permute-start(f32[16,3,128]{2,1,0:T(4,128)} %get-tuple-element.13), channel_id=1, source_target_pairs={{1,0},{2,1},{3,2},{4,3},{5,4},{6,5},{7,6},{0,7},{9,8},{10,9},{11,1... | collective-permute-start | bytes 73736 | tf_op jit(solution)/shard_map/ppermute | solution.py:515
  101.2 2.2 %copy-start = (f32[16,3,128]{2,1,0:T(4,128)}, f32[16,3,128]{2,1,0:T(4,128)S(1)}, u32[]{:S(2)}) copy-start(f32[16,3,128]{2,1,0:T(4,128)S(1)} %collective-permute-done.low) | copy-start | bytes 73732
  103.4 0.6 copy-start.1
  183.3 3.1 %collective-permute-start.2 = (f32[16,14,128]{2,1,0:T(8,128)S(1)}, f32[16,14,128]{2,1,0:T(8,128)S(1)}, u32[]{:S(2)}, u32[]{:S(2)}) collective-permute-start(f32[16,14,128]{2,1,0:T(8,128)S(1)} %pad_maximum_fusion), channel_id=1, source_target_pairs={{0,1},{1,2},{2,3},{3,4},{4,5},{5,6},{6,7},{7,0},{8,9},{9,10},{10,1... | collective-permute-start | bytes 344072 | tf_op jit(solution)/shard_map/ppermute | solution.py:515
  184.5 4.7 %collective-permute-start.3 = (f32[16,14,128]{2,1,0:T(8,128)S(1)}, f32[16,14,128]{2,1,0:T(8,128)S(1)}, u32[]{:S(2)}, u32[]{:S(2)}) collective-permute-start(f32[16,14,128]{2,1,0:T(8,128)S(1)} %pad_maximum_fusion.1), channel_id=1, source_target_pairs={{1,0},{2,1},{3,2},{4,3},{5,4},{6,5},{7,6},{0,7},{9,8},{10,9},{11,1... | collective-permute-start | bytes 344072 | tf_op jit(solution)/shard_map/ppermute | solution.py:515

commit v3 on v2

--- a/solution.py
+++ b/solution.py
@@ -52,10 +52,9 @@
 
 
 def pack_kernel(
-    place_ref, h_in, p_in, target_ref, flag_ref, out, here_ref, h_ref, p_ref, o_ref, tag_ref, h_sem, p_sem, o_sem, tag_sem
+    h_in, p_in, target_ref, flag_ref, out, h_ref, p_ref, o_ref, tag_ref, h_sem, p_sem, o_sem, tag_sem
 ):
     slots = target_ref.shape[1]
-    here_ref[0] = place_ref[0]
 
     def load(s):
         return (
@@ -72,6 +71,8 @@
             copy.start()
     tag_ref[:, 0:1, 0:slots] = jnp.broadcast_to(target_ref[...].astype(jnp.float32), (BS, 1, slots))
     tag_ref[:, 1:2, 0:slots] = jnp.broadcast_to(flag_ref[...].astype(jnp.float32), (BS, 1, slots))
+    for i in range(BS):
+        tag_ref[i, 2:3, :] = jnp.full((1, LANES), i, jnp.float32)
     tags = pltpu.make_async_copy(tag_ref, out.at[:, pl.ds(slots * SLOT_ROWS, 8), :], tag_sem)
     tags.start()
 
@@ -105,16 +106,13 @@
     return jnp.where(row >= 6, pltpu.roll(far, 6, 0), pltpu.roll(near, 6, 0))
 
 
-def pack(place, hydro, phase, targets, flags):
+def pack(hydro, phase, targets, flags):
     slots = hydro.shape[0]
     return pl.pallas_call(
         pack_kernel,
-        in_specs=[SMEM, ANY, ANY, WHOLE, WHOLE],
-        out_specs=[ANY, SMEM],
-        out_shape=[
-            made(BS, slots * SLOT_ROWS + 8, LANES),
-            jax.ShapeDtypeStruct((1,), jnp.int32),
-        ],
+        in_specs=[ANY, ANY, WHOLE, WHOLE],
+        out_specs=ANY,
+        out_shape=made(BS, slots * SLOT_ROWS + 8, LANES),
         scratch_shapes=[
             buffer(slots, 27, 32, LANES),
             buffer(slots, 15, 32, LANES),
@@ -126,7 +124,7 @@
             pltpu.SemaphoreType.DMA,
         ],
         compiler_params=room(60),
-    )(place, hydro.reshape(slots, 27, 32, LANES), phase.reshape(slots, 15, 32, LANES), targets, flags)
+    )(hydro.reshape(slots, 27, 32, LANES), phase.reshape(slots, 15, 32, LANES), targets, flags)
 
 
 def swap_bits(values, axis, unit):
@@ -166,7 +164,9 @@
 GROUPS += [[39, 40, 41, 42], [24, 25, 26, 43]]
 
 
-def survey_kernel(got, code_ref, sum_ref, up_ref, down_ref, tag_ref, b_ref, code_s, tag_sem, b_sem, code_sem):
+def survey_kernel(
+    got, code_ref, sum_ref, up_ref, down_ref, tag_ref, b_ref, code_s, tag_sem, b_sem, code_sem
+):
     slots = b_ref.shape[0]
     tags = pltpu.make_async_copy(got.at[:, pl.ds(slots * SLOT_ROWS, 8), :], tag_ref, tag_sem)
     tags.start()
@@ -189,7 +189,8 @@
             match = jnp.broadcast_to(label[:, t : t + 1], (8, LANES)) == value
             entry = sender + (2.0 * t + jnp.broadcast_to(flag[:, t : t + 1], (8, LANES)))
             code = code + jnp.where(match, entry, 0.0)
-    code_ref[...] = jnp.sum(code, axis=0, keepdims=True).astype(jnp.int32)
+    code_ref[0:1, :] = jnp.sum(code, axis=0, keepdims=True).astype(jnp.int32)
+    code_ref[1:2, :] = tag_ref[0, 2:3, :].astype(jnp.int32)
     table = pltpu.make_async_copy(code_ref, code_s, code_sem)
     table.start()
     table.wait()
@@ -224,7 +225,7 @@
         in_specs=[ANY],
         out_specs=[WHOLE, WHOLE, WHOLE, WHOLE],
         out_shape=[
-            jax.ShapeDtypeStruct((1, LANES), jnp.int32),
+            jax.ShapeDtypeStruct((2, LANES), jnp.int32),
             made(16, 3, BS, LANES),
             made(16, 3, LANES),
             made(16, 3, LANES),
@@ -232,7 +233,7 @@
         scratch_shapes=[
             buffer(16, 8, LANES),
             buffer(slots, 16, 40, LANES),
-            pltpu.SMEM((1, LANES), jnp.int32),
+            pltpu.SMEM((2, LANES), jnp.int32),
             pltpu.SemaphoreType.DMA,
             pltpu.SemaphoreType.DMA((slots,)),
             pltpu.SemaphoreType.DMA,
@@ -308,10 +309,10 @@
 
 
 def collide_kernel(
-    place_ref, rate_ref, code_ref, got, sums, low, high, out,
+    rate_ref, code_ref, got, sums, low, high, out,
     sum_ref, low_ref, high_ref, b_ref, n_ref, o_ref, side_sem, b_sem, o_sem,
 ):
-    place = place_ref[0]
+    place = code_ref[1, 0]
     sides = [
         pltpu.make_async_copy(a, b, side_sem.at[n])
         for n, (a, b) in enumerate(((sums, sum_ref), (low, low_ref), (high, high_ref)))
@@ -413,8 +414,6 @@
         back = from_moments(scaled)
 
         def put(kind, index, v, value):
-            if v[2] != 0:
-                value = pltpu.roll(value, v[2] % LANES, 1)
             out_ref[d, PLACE[kind, index], at, :] = value
 
         for q in range(27):
@@ -432,10 +431,10 @@
             put("p", k, SMALL[k], pop - (pop - equil) * (1.0 / 0.7))
 
 
-def collide(place, rates, code, got, sums, low, high):
+def collide(rates, code, got, sums, low, high):
     return pl.pallas_call(
         collide_kernel,
-        in_specs=[SMEM, SMEM, SMEM, ANY, ANY, ANY, ANY],
+        in_specs=[SMEM, SMEM, ANY, ANY, ANY, ANY],
         out_specs=ANY,
         out_shape=made(16, 42, BS, LANES),
         scratch_shapes=[
@@ -450,10 +449,10 @@
             pltpu.SemaphoreType.DMA((16, 3)),
         ],
         compiler_params=room(60),
-    )(place, rates, code, got, sums, low, high)
-
-
-def finish_kernel(got, low_ref, high_ref, hydro, phase, n_ref, h_ref, p_ref, n_sem, h_sem, p_sem):
+    )(rates, code, got, sums, low, high)
+
+
+def finish_kernel(got, low, high, hydro, phase, low_ref, high_ref, n_ref, h_ref, p_ref, side_sem, n_sem, h_sem, p_sem):
     row = lax.broadcasted_iota(jnp.int32, (BS, LANES), 0)
 
     def load(i):
@@ -467,8 +466,16 @@
             comps = pl.ds(group * 5, 5)
             yield pltpu.make_async_copy(p_ref.at[i, comps], phase.at[comps, x], p_sem.at[i, group])
 
+    sides = [
+        pltpu.make_async_copy(a, b, side_sem.at[n])
+        for n, (a, b) in enumerate(((low, low_ref), (high, high_ref)))
+    ]
+    for copy in sides:
+        copy.start()
     for i in range(16):
         load(i).start()
+    for copy in sides:
+        copy.wait()
 
     @pl.loop(0, 16)
     def _(i):
@@ -481,6 +488,8 @@
             elif v[1] == -1:
                 face = high_ref[i, pl.ds(DOWN_FACE.index(n), 1), :]
                 value = jnp.where(row == BS - 1, face, pltpu.roll(value, BS - 1, 0))
+            if v[2] != 0:
+                value = pltpu.roll(value, v[2] % LANES, 1)
             (h_ref if kind == "h" else p_ref)[i, index] = value
         for copy in leave(i):
             copy.start()
@@ -493,13 +502,16 @@
 def finish(got, low, high):
     return pl.pallas_call(
         finish_kernel,
-        in_specs=[ANY, WHOLE, WHOLE],
+        in_specs=[ANY, ANY, ANY],
         out_specs=[ANY, ANY],
         out_shape=[made(27, BS, BS, LANES), made(15, BS, BS, LANES)],
         scratch_shapes=[
+            buffer(16, 14, LANES),
+            buffer(16, 14, LANES),
             buffer(16, 42, BS, LANES),
             buffer(16, 27, BS, LANES),
             buffer(16, 15, BS, LANES),
+            pltpu.SemaphoreType.DMA((2,)),
             pltpu.SemaphoreType.DMA((16,)),
             pltpu.SemaphoreType.DMA((16, 3)),
             pltpu.SemaphoreType.DMA((16, 3)),
@@ -516,13 +528,12 @@
 
 
 def on_device(hydro_old, phase_old, targets, flags, relax_rates):
-    place = lax.axis_index("gx").astype(jnp.int32).reshape(1)
     slots = targets.shape[1]
-    packed, place = pack(place, hydro_old[0], phase_old[0], targets, flags)
+    packed = pack(hydro_old[0], phase_old[0], targets, flags)
     got = lax.all_to_all(packed, "gx", split_axis=0, concat_axis=0, tiled=True)
     code, sums, up, down = survey(got, slots)
     low, high = swap_faces(up, down)
-    send = collide(place, relax_rates, code, got, sums, low, high)
+    send = collide(relax_rates, code, got, sums, low, high)
     final = lax.all_to_all(send, "gx", split_axis=0, concat_axis=0, tiled=True)
     upper = jnp.concatenate([final[:, a:b, BS - 1, :] for a, b in runs(UP_FACE)], axis=1)
     lower = jnp.concatenate([final[:, a:b, 0, :] for a, b in runs(DOWN_FACE)], axis=1)

time: 195 us -> 193 us (0.990)
  no operation moved by 1% of the time
where the time goes in v3:
time: 193 us
  blocking collectives  151 us (78%)
  Pallas kernels  27 us (14%)
  waiting for transfers between devices  8 us (4%)
  starting transfers between devices  5.25 us (3%)
    all_to_all x1, blocking collectives, on_device(): got = lax.all_to_all(packed, 'gx', split_axis=0, concat_axis=0, tiled=True)  83 us
    all_to_all x1, blocking collectives, on_device(): final = lax.all_to_all(send, 'gx', split_axis=0, concat_axis=0, tiled=True)  68 us
    pallas_call x1, Pallas kernels, collide(): pl.pallas_call(collide_kernel, in_specs=[SMEM, SMEM, ANY, ANY, ANY, ANY],...  9.4 us
    ppermute x4, waiting for transfers between devices, swap_faces(): return (lax.ppermute(upper, 'gy', up), lax.ppermute(lower, 'gy', down))  8 us
    pallas_call x1, Pallas kernels, pack(): pl.pallas_call(pack_kernel, in_specs=[ANY, ANY, WHOLE, WHOLE], out_specs=...  6.45 us
    pallas_call x1, Pallas kernels, finish(): pl.pallas_call(finish_kernel, in_specs=[ANY, ANY, ANY], out_specs=[ANY, A...  5.8 us
    pallas_call x1, Pallas kernels, survey(): pl.pallas_call(survey_kernel, in_specs=[ANY], out_specs=[WHOLE, WHOLE, WH...  5.35 us
    ppermute x4, starting transfers between devices, swap_faces(): return (lax.ppermute(upper, 'gy', up), lax.ppermute(lower, 'gy', down))  5.25 us
  transfers between devices with their start and end apart: 4, of which 4 were waited for; matrix products, arithmetic and copies ran while one was open for 0% of the time, Pallas kernels for 0%

profile of v3, /device:TPU:1, one launch (start us, length us, event | category | flops | bytes accessed | tf_op | source)
XLA Modules:
  0.0 192.9 jit_solution(2133371138424050143)
XLA Ops:
  0.6 6.4 %shard_map.68 = f32[16,800,128]{2,1,0:T(8,128)} custom-call(f32[9,27,32,128]{3,2,1,0:T(8,128)} %bitcast.21, f32[9,15,32,128]{3,2,1,0:T(8,128)} %bitcast.22, s32[1,9]{1,0:T(1,128)} %target_ref.1, s32[1,9]{1,0:T(1,128)} %flag_ref.1), custom_call_target="tpu_custom_call" | custom-call | tf_op jit(solution)/shard_map/pallas_call | solution.py:111
  7.1 83.0 %all_to_all.10.got = f32[16,800,128]{2,1,0:T(8,128)} all-to-all(f32[16,800,128]{2,1,0:T(8,128)} %shard_map.68), channel_id=1, replica_groups=mesh['gx'=16,'gy'=8] {'gx'}, dimensions={0} | all-to-all | bytes 13107200 | tf_op jit(solution)/shard_map/all_to_all | solution.py:533
  90.1 5.4 %shard_map.69 = (s32[2,128]{1,0:T(2,128)}, f32[16,3,16,128]{3,2,1,0:T(8,128)}, f32[16,3,128]{2,1,0:T(4,128)}, f32[16,3,128]{2,1,0:T(4,128)}) custom-call(f32[16,800,128]{2,1,0:T(8,128)} %all_to_all.10.got), custom_call_target="tpu_custom_call" | custom-call | tf_op jit(solution)/shard_map/pallas_call | solution.py:223
  95.5 3.9 %collective-permute-start = (f32[16,3,128]{2,1,0:T(4,128)}, f32[16,3,128]{2,1,0:T(4,128)S(1)}, u32[]{:S(2)}, u32[]{:S(2)}) collective-permute-start(f32[16,3,128]{2,1,0:T(4,128)} %get-tuple-element.8), channel_id=1, source_target_pairs={{0,1},{1,2},{2,3},{3,4},{4,5},{5,6},{6,7},{7,0},{8,9},{9,10},{10,1... | collective-permute-start | bytes 73736 | tf_op jit(solution)/shard_map/ppermute | solution.py:527
  99.4 0.0 collective-permute-start.1
  99.4 1.3 collective-permute-done.low
  100.7 0.0 copy-start
  100.7 2.2 %collective-permute-done.1.high = f32[16,3,128]{2,1,0:T(4,128)S(1)} collective-permute-done((f32[16,3,128]{2,1,0:T(4,128)}, f32[16,3,128]{2,1,0:T(4,128)S(1)}, u32[]{:S(2)}, u32[]{:S(2)}) %collective-permute-start.1) | collective-permute-done | bytes 24608 | tf_op jit(solution)/shard_map/ppermute | solution.py:527
  102.9 0.0 copy-start.1
  102.9 0.0 copy-done
  102.9 0.6 copy-done.1
  103.5 9.4 %shard_map.70 = f32[16,42,16,128]{3,2,1,0:T(8,128)} custom-call(f32[27]{0:T(128)} %rate_ref.1, s32[2,128]{1,0:T(2,128)} %get-tuple-element.6.code_ref, f32[16,800,128]{2,1,0:T(8,128)} %all_to_all.10.got, f32[16,3,16,128]{3,2,1,0:T(8,128)} %get-tuple-element.7.sums, f32[16,3,128]{2,1,0:T(4,128)} %copy-done, f32[16,3,128]{2,1,0:T(4,128)} %copy-done.1), custom_call_target="tpu_custom_call" | custom-call | tf_op jit(solution)/shard_map/pallas_call | solution.py:435
  112.9 68.0 %all_to_all.11.got = f32[16,42,16,128]{3,2,1,0:T(8,128)S(1)} all-to-all(f32[16,42,16,128]{3,2,1,0:T(8,128)} %shard_map.70), channel_id=1, replica_groups=mesh['gx'=16,'gy'=8] {'gx'}, dimensions={0} | all-to-all | bytes 11010048 | tf_op jit(solution)/shard_map/all_to_all | solution.py:537
  181.0 0.1 fusion
  181.2 1.1 collective-permute-start.2
  182.4 0.2 collective-permute-start.3
  182.6 1.6 collective-permute-done.2.low
  184.3 2.8 %collective-permute-done.3.high = f32[16,14,128]{2,1,0:T(8,128)S(1)} collective-permute-done((f32[16,14,128]{2,1,0:T(8,128)S(1)}, f32[16,14,128]{2,1,0:T(8,128)S(1)}, u32[]{:S(2)}, u32[]{:S(2)}) %collective-permute-start.3) | collective-permute-done | bytes 114720 | tf_op jit(solution)/shard_map/ppermute | solution.py:527
  187.1 5.8 %shard_map.71 = (f32[27,16,16,128]{3,2,1,0:T(8,128)}, f32[15,16,16,128]{3,2,1,0:T(8,128)}) custom-call(f32[16,42,16,128]{3,2,1,0:T(8,128)S(1)} %all_to_all.11.got, f32[16,14,128]{2,1,0:T(8,128)S(1)} %collective-permute-done.2.low, f32[16,14,128]{2,1,0:T(8,128)S(1)} %collective-permute-done.3.high), custom_call_target="tpu_custom_call" | custom-call | tf_op jit(solution)/shard_map/pallas_call | solution.py:503
  (8 shorter events, 0.2 us)
Async XLA Ops:
  95.5 5.2 %collective-permute-start = (f32[16,3,128]{2,1,0:T(4,128)}, f32[16,3,128]{2,1,0:T(4,128)S(1)}, u32[]{:S(2)}, u32[]{:S(2)}) collective-permute-start(f32[16,3,128]{2,1,0:T(4,128)} %get-tuple-element.8), channel_id=1, source_target_pairs={{0,1},{1,2},{2,3},{3,4},{4,5},{5,6},{6,7},{7,0},{8,9},{9,10},{10,1... | collective-permute-start | bytes 73736 | tf_op jit(solution)/shard_map/ppermute | solution.py:527
  99.4 3.6 %collective-permute-start.1 = (f32[16,3,128]{2,1,0:T(4,128)}, f32[16,3,128]{2,1,0:T(4,128)S(1)}, u32[]{:S(2)}, u32[]{:S(2)}) collective-permute-start(f32[16,3,128]{2,1,0:T(4,128)} %get-tuple-element.9), channel_id=1, source_target_pairs={{1,0},{2,1},{3,2},{4,3},{5,4},{6,5},{7,6},{0,7},{9,8},{10,9},{11,1... | collective-permute-start | bytes 73736 | tf_op jit(solution)/shard_map/ppermute | solution.py:527
  100.7 2.2 %copy-start = (f32[16,3,128]{2,1,0:T(4,128)}, f32[16,3,128]{2,1,0:T(4,128)S(1)}, u32[]{:S(2)}) copy-start(f32[16,3,128]{2,1,0:T(4,128)S(1)} %collective-permute-done.low) | copy-start | bytes 73732
  102.9 0.6 copy-start.1
  181.2 3.1 %collective-permute-start.2 = (f32[16,14,128]{2,1,0:T(8,128)S(1)}, f32[16,14,128]{2,1,0:T(8,128)S(1)}, u32[]{:S(2)}, u32[]{:S(2)}) collective-permute-start(f32[16,14,128]{2,1,0:T(8,128)S(1)} %pad_maximum_fusion), channel_id=1, source_target_pairs={{0,1},{1,2},{2,3},{3,4},{4,5},{5,6},{6,7},{7,0},{8,9},{9,10},{10,1... | collective-permute-start | bytes 344072 | tf_op jit(solution)/shard_map/ppermute | solution.py:527
  182.4 4.7 %collective-permute-start.3 = (f32[16,14,128]{2,1,0:T(8,128)S(1)}, f32[16,14,128]{2,1,0:T(8,128)S(1)}, u32[]{:S(2)}, u32[]{:S(2)}) collective-permute-start(f32[16,14,128]{2,1,0:T(8,128)S(1)} %pad_maximum_fusion.1), channel_id=1, source_target_pairs={{1,0},{2,1},{3,2},{4,3},{5,4},{6,5},{7,6},{0,7},{9,8},{10,9},{11,1... | collective-permute-start | bytes 344072 | tf_op jit(solution)/shard_map/ppermute | solution.py:527

commit v4 on v3

--- a/solution.py
+++ b/solution.py
@@ -197,7 +197,7 @@
     for copy in loads:
         copy.wait()
 
-    @pl.loop(0, 16)
+    @pl.loop(0, 16, unroll=4)
     def _(d):
         values = []
         for level in range(8):

time: 193 us -> 192 us (level)
  no operation moved by 1% of the time
where the time goes in v4:
time: 192 us
  blocking collectives  151 us (79%)
  Pallas kernels  25.8 us (13%)
  waiting for transfers between devices  7.99 us (4%)
  starting transfers between devices  5.26 us (3%)
    all_to_all x1, blocking collectives, on_device(): got = lax.all_to_all(packed, 'gx', split_axis=0, concat_axis=0, tiled=True)  83 us
    all_to_all x1, blocking collectives, on_device(): final = lax.all_to_all(send, 'gx', split_axis=0, concat_axis=0, tiled=True)  68 us
    pallas_call x1, Pallas kernels, collide(): pl.pallas_call(collide_kernel, in_specs=[SMEM, SMEM, ANY, ANY, ANY, ANY],...  9.4 us
    ppermute x4, waiting for transfers between devices, swap_faces(): return (lax.ppermute(upper, 'gy', up), lax.ppermute(lower, 'gy', down))  7.99 us
    pallas_call x1, Pallas kernels, pack(): pl.pallas_call(pack_kernel, in_specs=[ANY, ANY, WHOLE, WHOLE], out_specs=...  6.45 us
    pallas_call x1, Pallas kernels, finish(): pl.pallas_call(finish_kernel, in_specs=[ANY, ANY, ANY], out_specs=[ANY, A...  5.8 us
    ppermute x4, starting transfers between devices, swap_faces(): return (lax.ppermute(upper, 'gy', up), lax.ppermute(lower, 'gy', down))  5.26 us
    pallas_call x1, Pallas kernels, survey(): pl.pallas_call(survey_kernel, in_specs=[ANY], out_specs=[WHOLE, WHOLE, WH...  4.19 us
  transfers between devices with their start and end apart: 4, of which 4 were waited for; matrix products, arithmetic and copies ran while one was open for 0% of the time, Pallas kernels for 0%

profile of v4, /device:TPU:1, one launch (start us, length us, event | category | flops | bytes accessed | tf_op | source)
XLA Modules:
  0.0 191.7 jit_solution(9595919834324886416)
XLA Ops:
  0.6 6.4 %shard_map.68 = f32[16,800,128]{2,1,0:T(8,128)} custom-call(f32[9,27,32,128]{3,2,1,0:T(8,128)} %bitcast.21, f32[9,15,32,128]{3,2,1,0:T(8,128)} %bitcast.22, s32[1,9]{1,0:T(1,128)} %target_ref.1, s32[1,9]{1,0:T(1,128)} %flag_ref.1), custom_call_target="tpu_custom_call" | custom-call | tf_op jit(solution)/shard_map/pallas_call | solution.py:111
  7.1 83.0 %all_to_all.10.got = f32[16,800,128]{2,1,0:T(8,128)} all-to-all(f32[16,800,128]{2,1,0:T(8,128)} %shard_map.68), channel_id=1, replica_groups=mesh['gx'=16,'gy'=8] {'gx'}, dimensions={0} | all-to-all | bytes 13107200 | tf_op jit(solution)/shard_map/all_to_all | solution.py:533
  90.1 4.2 %shard_map.69 = (s32[2,128]{1,0:T(2,128)}, f32[16,3,16,128]{3,2,1,0:T(8,128)}, f32[16,3,128]{2,1,0:T(4,128)}, f32[16,3,128]{2,1,0:T(4,128)}) custom-call(f32[16,800,128]{2,1,0:T(8,128)} %all_to_all.10.got), custom_call_target="tpu_custom_call" | custom-call | tf_op jit(solution)/shard_map/pallas_call | solution.py:223
  94.3 3.9 %collective-permute-start = (f32[16,3,128]{2,1,0:T(4,128)}, f32[16,3,128]{2,1,0:T(4,128)S(1)}, u32[]{:S(2)}, u32[]{:S(2)}) collective-permute-start(f32[16,3,128]{2,1,0:T(4,128)} %get-tuple-element.8), channel_id=1, source_target_pairs={{0,1},{1,2},{2,3},{3,4},{4,5},{5,6},{6,7},{7,0},{8,9},{9,10},{10,1... | collective-permute-start | bytes 73736 | tf_op jit(solution)/shard_map/ppermute | solution.py:527
  98.2 0.0 collective-permute-start.1
  98.2 1.3 collective-permute-done.low
  99.5 0.0 copy-start
  99.5 2.2 %collective-permute-done.1.high = f32[16,3,128]{2,1,0:T(4,128)S(1)} collective-permute-done((f32[16,3,128]{2,1,0:T(4,128)}, f32[16,3,128]{2,1,0:T(4,128)S(1)}, u32[]{:S(2)}, u32[]{:S(2)}) %collective-permute-start.1) | collective-permute-done | bytes 24608 | tf_op jit(solution)/shard_map/ppermute | solution.py:527
  101.7 0.0 copy-start.1
  101.7 0.0 copy-done
  101.7 0.6 copy-done.1
  102.3 9.4 %shard_map.70 = f32[16,42,16,128]{3,2,1,0:T(8,128)} custom-call(f32[27]{0:T(128)} %rate_ref.1, s32[2,128]{1,0:T(2,128)} %get-tuple-element.6.code_ref, f32[16,800,128]{2,1,0:T(8,128)} %all_to_all.10.got, f32[16,3,16,128]{3,2,1,0:T(8,128)} %get-tuple-element.7.sums, f32[16,3,128]{2,1,0:T(4,128)} %copy-done, f32[16,3,128]{2,1,0:T(4,128)} %copy-done.1), custom_call_target="tpu_custom_call" | custom-call | tf_op jit(solution)/shard_map/pallas_call | solution.py:435
  111.8 68.0 %all_to_all.11.got = f32[16,42,16,128]{3,2,1,0:T(8,128)S(1)} all-to-all(f32[16,42,16,128]{3,2,1,0:T(8,128)} %shard_map.70), channel_id=1, replica_groups=mesh['gx'=16,'gy'=8] {'gx'}, dimensions={0} | all-to-all | bytes 11010048 | tf_op jit(solution)/shard_map/all_to_all | solution.py:537
  179.8 0.1 fusion
  180.0 1.1 collective-permute-start.2
  181.2 0.3 collective-permute-start.3
  181.5 1.6 collective-permute-done.2.low
  183.1 2.8 %collective-permute-done.3.high = f32[16,14,128]{2,1,0:T(8,128)S(1)} collective-permute-done((f32[16,14,128]{2,1,0:T(8,128)S(1)}, f32[16,14,128]{2,1,0:T(8,128)S(1)}, u32[]{:S(2)}, u32[]{:S(2)}) %collective-permute-start.3) | collective-permute-done | bytes 114720 | tf_op jit(solution)/shard_map/ppermute | solution.py:527
  185.9 5.8 %shard_map.71 = (f32[27,16,16,128]{3,2,1,0:T(8,128)}, f32[15,16,16,128]{3,2,1,0:T(8,128)}) custom-call(f32[16,42,16,128]{3,2,1,0:T(8,128)S(1)} %all_to_all.11.got, f32[16,14,128]{2,1,0:T(8,128)S(1)} %collective-permute-done.2.low, f32[16,14,128]{2,1,0:T(8,128)S(1)} %collective-permute-done.3.high), custom_call_target="tpu_custom_call" | custom-call | tf_op jit(solution)/shard_map/pallas_call | solution.py:503
  (8 shorter events, 0.2 us)
Async XLA Ops:
  94.3 5.2 %collective-permute-start = (f32[16,3,128]{2,1,0:T(4,128)}, f32[16,3,128]{2,1,0:T(4,128)S(1)}, u32[]{:S(2)}, u32[]{:S(2)}) collective-permute-start(f32[16,3,128]{2,1,0:T(4,128)} %get-tuple-element.8), channel_id=1, source_target_pairs={{0,1},{1,2},{2,3},{3,4},{4,5},{5,6},{6,7},{7,0},{8,9},{9,10},{10,1... | collective-permute-start | bytes 73736 | tf_op jit(solution)/shard_map/ppermute | solution.py:527
  98.2 3.6 %collective-permute-start.1 = (f32[16,3,128]{2,1,0:T(4,128)}, f32[16,3,128]{2,1,0:T(4,128)S(1)}, u32[]{:S(2)}, u32[]{:S(2)}) collective-permute-start(f32[16,3,128]{2,1,0:T(4,128)} %get-tuple-element.9), channel_id=1, source_target_pairs={{1,0},{2,1},{3,2},{4,3},{5,4},{6,5},{7,6},{0,7},{9,8},{10,9},{11,1... | collective-permute-start | bytes 73736 | tf_op jit(solution)/shard_map/ppermute | solution.py:527
  99.5 2.2 %copy-start = (f32[16,3,128]{2,1,0:T(4,128)}, f32[16,3,128]{2,1,0:T(4,128)S(1)}, u32[]{:S(2)}) copy-start(f32[16,3,128]{2,1,0:T(4,128)S(1)} %collective-permute-done.low) | copy-start | bytes 73732
  101.7 0.6 copy-start.1
  180.0 3.1 %collective-permute-start.2 = (f32[16,14,128]{2,1,0:T(8,128)S(1)}, f32[16,14,128]{2,1,0:T(8,128)S(1)}, u32[]{:S(2)}, u32[]{:S(2)}) collective-permute-start(f32[16,14,128]{2,1,0:T(8,128)S(1)} %pad_maximum_fusion), channel_id=1, source_target_pairs={{0,1},{1,2},{2,3},{3,4},{4,5},{5,6},{6,7},{7,0},{8,9},{9,10},{10,1... | collective-permute-start | bytes 344072 | tf_op jit(solution)/shard_map/ppermute | solution.py:527
  181.2 4.7 %collective-permute-start.3 = (f32[16,14,128]{2,1,0:T(8,128)S(1)}, f32[16,14,128]{2,1,0:T(8,128)S(1)}, u32[]{:S(2)}, u32[]{:S(2)}) collective-permute-start(f32[16,14,128]{2,1,0:T(8,128)S(1)} %pad_maximum_fusion.1), channel_id=1, source_target_pairs={{1,0},{2,1},{3,2},{4,3},{5,4},{6,5},{7,6},{0,7},{9,8},{10,9},{11,1... | collective-permute-start | bytes 344072 | tf_op jit(solution)/shard_map/ppermute | solution.py:527

commit v5 on v4

--- a/solution.py
+++ b/solution.py
@@ -458,13 +458,22 @@
     def load(i):
         return pltpu.make_async_copy(got.at[i], n_ref.at[i], n_sem.at[i])
 
-    def leave(i):
+    leave = []
+    for part in range(4):
+        copies = []
         for group in range(3):
-            x = (i + group + 15) % 16
-            comps = pl.ds(group * 9, 9)
-            yield pltpu.make_async_copy(h_ref.at[i, comps], hydro.at[comps, x], h_sem.at[i, group])
-            comps = pl.ds(group * 5, 5)
-            yield pltpu.make_async_copy(p_ref.at[i, comps], phase.at[comps, x], p_sem.at[i, group])
+            first = part * 4 + group - 1
+            cuts = ((first, 4),)
+            if first < 0:
+                cuts = ((15, 1), (0, 3))
+            elif first > 12:
+                cuts = ((13, 3), (0, 1))
+            for x, count in cuts:
+                at = len(copies)
+                for source, to, width, sem in ((h_ref, hydro, 9, h_sem), (p_ref, phase, 5, p_sem)):
+                    box = (pl.ds(group * width, width), pl.ds(x, count))
+                    copies.append(pltpu.make_async_copy(source.at[box], to.at[box], sem.at[part, at]))
+        leave.append(copies)
 
     sides = [
         pltpu.make_async_copy(a, b, side_sem.at[n])
@@ -477,8 +486,7 @@
     for copy in sides:
         copy.wait()
 
-    @pl.loop(0, 16)
-    def _(i):
+    def plane(i):
         load(i).wait()
         for n, (kind, index, v) in enumerate(ORDER):
             value = n_ref[i, n]
@@ -490,12 +498,14 @@
                 value = jnp.where(row == BS - 1, face, pltpu.roll(value, BS - 1, 0))
             if v[2] != 0:
                 value = pltpu.roll(value, v[2] % LANES, 1)
-            (h_ref if kind == "h" else p_ref)[i, index] = value
-        for copy in leave(i):
+            (h_ref if kind == "h" else p_ref)[index, (i + v[0]) & 15] = value
+
+    for part in range(4):
+        pl.loop(part * 4, part * 4 + 4)(plane)
+        for copy in leave[part]:
             copy.start()
-
-    for i in range(16):
-        for copy in leave(i):
+    for copies in leave:
+        for copy in copies:
             copy.wait()
 
 
@@ -509,12 +519,12 @@
             buffer(16, 14, LANES),
             buffer(16, 14, LANES),
             buffer(16, 42, BS, LANES),
-            buffer(16, 27, BS, LANES),
-            buffer(16, 15, BS, LANES),
+            buffer(27, BS, BS, LANES),
+            buffer(15, BS, BS, LANES),
             pltpu.SemaphoreType.DMA((2,)),
             pltpu.SemaphoreType.DMA((16,)),
-            pltpu.SemaphoreType.DMA((16, 3)),
-            pltpu.SemaphoreType.DMA((16, 3)),
+            pltpu.SemaphoreType.DMA((4, 8)),
+            pltpu.SemaphoreType.DMA((4, 8)),
         ],
         compiler_params=room(24),
     )(got, low, high)

time: 192 us -> 192 us (level)
  no operation moved by 1% of the time
where the time goes in v5:
time: 192 us
  blocking collectives  151 us (79%)
  Pallas kernels  25.8 us (13%)
  waiting for transfers between devices  7.99 us (4%)
  starting transfers between devices  5.25 us (3%)
    all_to_all x1, blocking collectives, on_device(): got = lax.all_to_all(packed, 'gx', split_axis=0, concat_axis=0, tiled=True)  83 us
    all_to_all x1, blocking collectives, on_device(): final = lax.all_to_all(send, 'gx', split_axis=0, concat_axis=0, tiled=True)  68 us
    pallas_call x1, Pallas kernels, collide(): pl.pallas_call(collide_kernel, in_specs=[SMEM, SMEM, ANY, ANY, ANY, ANY],...  9.4 us
    ppermute x4, waiting for transfers between devices, swap_faces(): return (lax.ppermute(upper, 'gy', up), lax.ppermute(lower, 'gy', down))  7.99 us
    pallas_call x1, Pallas kernels, pack(): pl.pallas_call(pack_kernel, in_specs=[ANY, ANY, WHOLE, WHOLE], out_specs=...  6.45 us
    pallas_call x1, Pallas kernels, finish(): pl.pallas_call(finish_kernel, in_specs=[ANY, ANY, ANY], out_specs=[ANY, A...  5.8 us
    ppermute x4, starting transfers between devices, swap_faces(): return (lax.ppermute(upper, 'gy', up), lax.ppermute(lower, 'gy', down))  5.25 us
    pallas_call x1, Pallas kernels, survey(): pl.pallas_call(survey_kernel, in_specs=[ANY], out_specs=[WHOLE, WHOLE, WH...  4.19 us
  transfers between devices with their start and end apart: 4, of which 4 were waited for; matrix products, arithmetic and copies ran while one was open for 0% of the time, Pallas kernels for 0%

profile of v5, /device:TPU:1, one launch (start us, length us, event | category | flops | bytes accessed | tf_op | source)
XLA Modules:
  0.0 191.7 jit_solution(4392297291155398290)
XLA Ops:
  0.6 6.4 %shard_map.68 = f32[16,800,128]{2,1,0:T(8,128)} custom-call(f32[9,27,32,128]{3,2,1,0:T(8,128)} %bitcast.21, f32[9,15,32,128]{3,2,1,0:T(8,128)} %bitcast.22, s32[1,9]{1,0:T(1,128)} %target_ref.1, s32[1,9]{1,0:T(1,128)} %flag_ref.1), custom_call_target="tpu_custom_call" | custom-call | tf_op jit(solution)/shard_map/pallas_call | solution.py:111
  7.1 83.0 %all_to_all.10.got = f32[16,800,128]{2,1,0:T(8,128)} all-to-all(f32[16,800,128]{2,1,0:T(8,128)} %shard_map.68), channel_id=1, replica_groups=mesh['gx'=16,'gy'=8] {'gx'}, dimensions={0} | all-to-all | bytes 13107200 | tf_op jit(solution)/shard_map/all_to_all | solution.py:543
  90.1 4.2 %shard_map.69 = (s32[2,128]{1,0:T(2,128)}, f32[16,3,16,128]{3,2,1,0:T(8,128)}, f32[16,3,128]{2,1,0:T(4,128)}, f32[16,3,128]{2,1,0:T(4,128)}) custom-call(f32[16,800,128]{2,1,0:T(8,128)} %all_to_all.10.got), custom_call_target="tpu_custom_call" | custom-call | tf_op jit(solution)/shard_map/pallas_call | solution.py:223
  94.3 3.9 %collective-permute-start = (f32[16,3,128]{2,1,0:T(4,128)}, f32[16,3,128]{2,1,0:T(4,128)S(1)}, u32[]{:S(2)}, u32[]{:S(2)}) collective-permute-start(f32[16,3,128]{2,1,0:T(4,128)} %get-tuple-element.8), channel_id=1, source_target_pairs={{0,1},{1,2},{2,3},{3,4},{4,5},{5,6},{6,7},{7,0},{8,9},{9,10},{10,1... | collective-permute-start | bytes 73736 | tf_op jit(solution)/shard_map/ppermute | solution.py:537
  98.2 0.0 collective-permute-start.1
  98.2 1.3 collective-permute-done.low
  99.5 0.0 copy-start
  99.5 2.2 %collective-permute-done.1.high = f32[16,3,128]{2,1,0:T(4,128)S(1)} collective-permute-done((f32[16,3,128]{2,1,0:T(4,128)}, f32[16,3,128]{2,1,0:T(4,128)S(1)}, u32[]{:S(2)}, u32[]{:S(2)}) %collective-permute-start.1) | collective-permute-done | bytes 24608 | tf_op jit(solution)/shard_map/ppermute | solution.py:537
  101.7 0.0 copy-start.1
  101.7 0.0 copy-done
  101.7 0.6 copy-done.1
  102.3 9.4 %shard_map.70 = f32[16,42,16,128]{3,2,1,0:T(8,128)} custom-call(f32[27]{0:T(128)} %rate_ref.1, s32[2,128]{1,0:T(2,128)} %get-tuple-element.6.code_ref, f32[16,800,128]{2,1,0:T(8,128)} %all_to_all.10.got, f32[16,3,16,128]{3,2,1,0:T(8,128)} %get-tuple-element.7.sums, f32[16,3,128]{2,1,0:T(4,128)} %copy-done, f32[16,3,128]{2,1,0:T(4,128)} %copy-done.1), custom_call_target="tpu_custom_call" | custom-call | tf_op jit(solution)/shard_map/pallas_call | solution.py:435
  111.8 68.0 %all_to_all.11.got = f32[16,42,16,128]{3,2,1,0:T(8,128)S(1)} all-to-all(f32[16,42,16,128]{3,2,1,0:T(8,128)} %shard_map.70), channel_id=1, replica_groups=mesh['gx'=16,'gy'=8] {'gx'}, dimensions={0} | all-to-all | bytes 11010048 | tf_op jit(solution)/shard_map/all_to_all | solution.py:547
  179.8 0.1 fusion
  180.0 1.1 collective-permute-start.2
  181.2 0.3 collective-permute-start.3
  181.5 1.6 collective-permute-done.2.low
  183.1 2.8 %collective-permute-done.3.high = f32[16,14,128]{2,1,0:T(8,128)S(1)} collective-permute-done((f32[16,14,128]{2,1,0:T(8,128)S(1)}, f32[16,14,128]{2,1,0:T(8,128)S(1)}, u32[]{:S(2)}, u32[]{:S(2)}) %collective-permute-start.3) | collective-permute-done | bytes 114720 | tf_op jit(solution)/shard_map/ppermute | solution.py:537
  185.9 5.8 %shard_map.71 = (f32[27,16,16,128]{3,2,1,0:T(8,128)}, f32[15,16,16,128]{3,2,1,0:T(8,128)}) custom-call(f32[16,42,16,128]{3,2,1,0:T(8,128)S(1)} %all_to_all.11.got, f32[16,14,128]{2,1,0:T(8,128)S(1)} %collective-permute-done.2.low, f32[16,14,128]{2,1,0:T(8,128)S(1)} %collective-permute-done.3.high), custom_call_target="tpu_custom_call" | custom-call | tf_op jit(solution)/shard_map/pallas_call | solution.py:513
  (8 shorter events, 0.2 us)
Async XLA Ops:
  94.3 5.2 %collective-permute-start = (f32[16,3,128]{2,1,0:T(4,128)}, f32[16,3,128]{2,1,0:T(4,128)S(1)}, u32[]{:S(2)}, u32[]{:S(2)}) collective-permute-start(f32[16,3,128]{2,1,0:T(4,128)} %get-tuple-element.8), channel_id=1, source_target_pairs={{0,1},{1,2},{2,3},{3,4},{4,5},{5,6},{6,7},{7,0},{8,9},{9,10},{10,1... | collective-permute-start | bytes 73736 | tf_op jit(solution)/shard_map/ppermute | solution.py:537
  98.2 3.6 %collective-permute-start.1 = (f32[16,3,128]{2,1,0:T(4,128)}, f32[16,3,128]{2,1,0:T(4,128)S(1)}, u32[]{:S(2)}, u32[]{:S(2)}) collective-permute-start(f32[16,3,128]{2,1,0:T(4,128)} %get-tuple-element.9), channel_id=1, source_target_pairs={{1,0},{2,1},{3,2},{4,3},{5,4},{6,5},{7,6},{0,7},{9,8},{10,9},{11,1... | collective-permute-start | bytes 73736 | tf_op jit(solution)/shard_map/ppermute | solution.py:537
  99.5 2.2 %copy-start = (f32[16,3,128]{2,1,0:T(4,128)}, f32[16,3,128]{2,1,0:T(4,128)S(1)}, u32[]{:S(2)}) copy-start(f32[16,3,128]{2,1,0:T(4,128)S(1)} %collective-permute-done.low) | copy-start | bytes 73732
  101.7 0.6 copy-start.1
  180.0 3.1 %collective-permute-start.2 = (f32[16,14,128]{2,1,0:T(8,128)S(1)}, f32[16,14,128]{2,1,0:T(8,128)S(1)}, u32[]{:S(2)}, u32[]{:S(2)}) collective-permute-start(f32[16,14,128]{2,1,0:T(8,128)S(1)} %pad_maximum_fusion), channel_id=1, source_target_pairs={{0,1},{1,2},{2,3},{3,4},{4,5},{5,6},{6,7},{7,0},{8,9},{9,10},{10,1... | collective-permute-start | bytes 344072 | tf_op jit(solution)/shard_map/ppermute | solution.py:537
  181.2 4.7 %collective-permute-start.3 = (f32[16,14,128]{2,1,0:T(8,128)S(1)}, f32[16,14,128]{2,1,0:T(8,128)S(1)}, u32[]{:S(2)}, u32[]{:S(2)}) collective-permute-start(f32[16,14,128]{2,1,0:T(8,128)S(1)} %pad_maximum_fusion.1), channel_id=1, source_target_pairs={{1,0},{2,1},{3,2},{4,3},{5,4},{6,5},{7,6},{0,7},{9,8},{10,9},{11,1... | collective-permute-start | bytes 344072 | tf_op jit(solution)/shard_map/ppermute | solution.py:537
